TPU v7x, 512 devices: a whole 4x8x8 slice. The times are simulated.
512 devices in a mesh: ctx: 32 (over y, x), head: 16 (over z, core).
Axes of the slice: x: 4, y: 8, z: 8, core: 2. Of those that a mesh axis runs over, the one named last changes fastest.
Arguments:
- queries: bfloat16 [16384, 8192], P('ctx', 'head'), may hold values from -2 to 2
- keys: bfloat16 [16384, 8192], P('ctx', 'head'), may hold values from -2 to 2
- values: bfloat16 [16384, 8192], P('ctx', 'head'), may hold values from -6 to 6
- out_grad: bfloat16 [16384, 8192], P('ctx', 'head'), may hold values from -6 to 6
- decay_rate: float32 [64], P('head'), may hold values from 3.0517578e-06 to 0.034, as said below
- gain: float32 [8192], P('head'), may hold values from 0.1 to 1.9
Outputs:
- normed: bfloat16 [16384, 8192], P('ctx', 'head')
- query_gradient: bfloat16 [16384, 8192], P('ctx', 'head')
- key_gradient: bfloat16 [16384, 8192], P('ctx', 'head')
- value_gradient: bfloat16 [16384, 8192], P('ctx', 'head')
Inputs may be any that keep to these rules, and one draw needn't show every extreme that they name: `decay_rate`: rates are positive.
All inputs are finite; a program needn't handle non-finite values.
Results may differ from a plain program's by a relative error of at most 0.0051.
Values sent between devices are 32-bit elements; how exact they have to be, the bound alone decides.
No kernel may reach another device: no remote copies, remote signals or barrier semaphores. Data moves between devices by JAX's collectives and lax.ppermute only.
A program may use at most 64 MiB of HBM per device.

v0:
```python
import jax
import jax.numpy as jnp
from jax import lax
from jax.sharding import PartitionSpec as P

DH = 128


def decay_table(rate, count):
    pos = jnp.arange(count, dtype=jnp.float32)
    diff = pos[:, None] - pos[None, :]
    return jnp.where(
        diff[None] >= 0, jnp.exp(-rate[:, None, None] * jnp.maximum(diff, 0.0)[None]), 0.0
    )


def folder(decay_rate, count, me, later, block_piece):
    rows = jnp.arange(block_piece.shape[0], dtype=jnp.float32)
    if later:
        gap = rows - me - 1.0
    else:
        gap = me - 1.0 - rows
    scale_factor = jnp.where(
        gap[:, None] >= 0,
        jnp.exp(-decay_rate[None, :] * count * jnp.maximum(gap, 0.0)[:, None]),
        0.0,
    )
    return jnp.einsum("ul,ulec->lec", scale_factor, block_piece, precision=lax.Precision.HIGHEST)


def local(queries, keys, values, out_grad, decay_rate, gain):
    highest_precision = lax.Precision.HIGHEST
    single_float = jnp.float32
    count = queries.shape[0]
    heads = decay_rate.shape[0]
    shape3 = (count, heads, DH)
    local_queries = queries.reshape(shape3)
    local_keys = keys.reshape(shape3)
    local_values = values.reshape(shape3)
    pos = jnp.arange(count, dtype=single_float)
    table = decay_table(decay_rate, count)
    start_weight = jnp.exp(-decay_rate[None, :] * (pos[:, None] + 1.0))[..., None]
    end_weight = jnp.exp(-decay_rate[None, :] * (count - 1.0 - pos[:, None]))[..., None]
    tail_weight = jnp.exp(-decay_rate[None, :] * (count - pos[:, None]))[..., None]
    head_weight = jnp.exp(-decay_rate[None, :] * pos[:, None])[..., None]
    me = lax.axis_index("ctx").astype(single_float)
    weights = (
        jnp.einsum("thd,shd->hts", local_queries, local_keys, preferred_element_type=single_float)
        * table
    ).astype(jnp.bfloat16)
    running_state = jnp.einsum(
        "ldg,ldj->dgj",
        local_keys.astype(single_float) * end_weight,
        local_values.astype(single_float),
        precision=highest_precision,
    )
    prefix_sum = folder(
        decay_rate, count, me, False, lax.all_gather(running_state[None], "ctx", axis=0, tiled=True)
    )
    attended_output = jnp.einsum(
        "hts,shd->thd", weights, local_values, preferred_element_type=single_float
    )
    attended_output = (
        attended_output
        + jnp.einsum(
            "web,ebo->weo",
            local_queries.astype(single_float),
            prefix_sum,
            precision=highest_precision,
        )
        * start_weight
    )
    attended_output = attended_output.reshape(count, heads * DH)
    scaled = out_grad.astype(single_float) * gain
    squares, crossing = lax.psum(
        (
            jnp.sum(attended_output * attended_output, axis=1),
            jnp.sum(scaled * attended_output, axis=1),
        ),
        "head",
    )
    total = float(heads * lax.axis_size("head") * DH)
    rinv = lax.rsqrt(squares / total + 1e-06)[:, None]
    cross = (crossing / total)[:, None]
    normed = (attended_output * rinv * gain).astype(jnp.bfloat16)
    attn_grad = (rinv * scaled - attended_output * (rinv * rinv * rinv * cross)).astype(
        jnp.bfloat16
    )
    local_decay = attn_grad.reshape(shape3)
    grad_state = jnp.einsum(
        "ldg,ldj->dgj",
        local_queries.astype(single_float) * head_weight,
        local_decay.astype(single_float),
        precision=highest_precision,
    )
    suffix_sum = folder(
        decay_rate, count, me, True, lax.all_gather(grad_state[None], "ctx", axis=0, tiled=True)
    )
    grad_weights = (
        jnp.einsum("thd,shd->hts", local_decay, local_values, preferred_element_type=single_float)
        * table
    ).astype(jnp.bfloat16)
    query_gradient = jnp.einsum(
        "hts,shd->thd", grad_weights, local_keys, preferred_element_type=single_float
    )
    query_gradient = (
        query_gradient
        + jnp.einsum(
            "dmq,msq->dms",
            local_decay.astype(single_float),
            prefix_sum,
            precision=highest_precision,
        )
        * start_weight
    )
    key_gradient = jnp.einsum(
        "hts,thd->shd", grad_weights, local_queries, preferred_element_type=single_float
    )
    key_gradient = (
        key_gradient
        + jnp.einsum(
            "noq,ofq->nof",
            local_values.astype(single_float),
            suffix_sum,
            precision=highest_precision,
        )
        * tail_weight
    )
    value_gradient = jnp.einsum(
        "hts,thd->shd", weights, local_decay, preferred_element_type=single_float
    )
    value_gradient = (
        value_gradient
        + jnp.einsum(
            "dyp,ypn->dyn", local_keys.astype(single_float), suffix_sum, precision=highest_precision
        )
        * tail_weight
    )
    flat = (count, heads * DH)
    return (
        normed,
        query_gradient.astype(jnp.bfloat16).reshape(flat),
        key_gradient.astype(jnp.bfloat16).reshape(flat),
        value_gradient.astype(jnp.bfloat16).reshape(flat),
    )


def solution(mesh):
    return jax.shard_map(
        local,
        mesh=mesh,
        in_specs=(
            P("ctx", "head"),
            P("ctx", "head"),
            P("ctx", "head"),
            P("ctx", "head"),
            P("head"),
            P("head"),
        ),
        out_specs=(P("ctx", "head"), P("ctx", "head"), P("ctx", "head"), P("ctx", "head")),
        check_vma=False,
    )
```

profile of v0, /device:TPU:1, one launch (start us, length us, event | category | flops | bytes accessed | tf_op | source)
XLA Modules:
  0.0 277.7 jit_solution(4611358350097359607)
XLA Ops:
  7.2 0.0 copy-start
  7.2 0.0 copy-start.8
  7.2 0.0 all-gather.5.cloned.1.call-start
  7.3 0.7 broadcast_multiply_fusion
  8.0 1.3 copy.100
  9.3 0.0 copy-start.7
  9.3 0.1 multiply_exponential_fusion
  9.4 0.0 copy-done
  9.4 1.4 fusion.16
  10.7 0.0 all-gather.5.cloned.1.call-update
  10.8 0.0 all-gather.7.cloned.1.call-start
  10.9 0.1 select_bitcast_fusion
  11.0 0.1 copy.58
  11.0 1.3 copy.70
  12.3 0.3 fusion.20
  12.6 0.0 copy-start.11
  12.6 0.2 fusion.19
  12.7 0.0 copy-start.10
  12.8 0.0 copy-done.8
  12.8 1.4 multiply_convert_fusion.1
  14.2 1.4 copy-done.1
  15.6 0.8 convolution_bitcast_fusion.3
  16.4 103.9 %all-gather.5.cloned.1.call-done = f32[128,128,128]{2,1,0:T(8,128)} async-done(((f32[4,128,128]{2,1,0:T(8,128)}), f32[128,128,128]{2,1,0:T(8,128)}) %all-gather.5.cloned.1.call-update) | async-done | bytes 8388624 | tf_op jit(solution)/shard_map/all_gather | solution.py:58
  120.3 12.0 %fusion = f32[4,1,128,128]{3,1,2,0:T(1,128)S(1)} fusion(f32[32,4,1,1]{0,2,3,1:T(1,128)S(1)} %copy.58, f32[32,4,128,128]{3,2,1,0:T(8,128)} %bitcast.110), kind=kOutput, calls=%fused_computation.1 | convolution fusion | flops 25165824 | bytes 8651264 | tf_op jit(solution)/shard_map/ul,ulec->lec/dot_general | solution.py:28
  132.3 0.0 copy-start.13
  132.4 0.7 multiply_reduce_fusion.2
  133.1 0.3 copy.41
  133.4 0.0 copy-start.12
  133.4 1.3 multiply_reduce_fusion.1
  134.7 25.3 %all-reduce = (f32[512]{0:T(512)S(1)}, f32[512]{0:T(512)S(1)}) all-reduce(f32[512]{0:T(512)S(1)} %get-tuple-element.26, f32[512]{0:T(512)S(1)} %multiply_reduce_fusion.1), channel_id=1, replica_groups=mesh['ctx'=32,'head'=16] {'head'}, use_global_device_ids=true, to_apply=%region_1.2 | all-reduce | flops 1024 | bytes 8192 | tf_op jit(solution)/shard_map/psum | solution.py:75
  160.0 2.2 subtract_convert_fusion
  162.2 0.2 copy.71
  162.4 0.0 copy-start.5
  162.4 1.4 fusion.13
  163.8 0.0 all-gather.7.cloned.1.call-update
  163.9 2.6 multiply_convert_fusion
  166.5 1.3 copy-done.3
  167.8 2.0 convolution_bitcast_fusion.2
  169.8 2.5 fusion.10
  172.2 2.0 copy.55
  174.3 2.7 convolution_bitcast_fusion.1
  177.0 0.4 convolution_bitcast_fusion
  177.4 86.0 %all-gather.7.cloned.1.call-done = f32[128,128,128]{2,1,0:T(8,128)} async-done(((f32[4,128,128]{2,1,0:T(8,128)}), f32[128,128,128]{2,1,0:T(8,128)}) %all-gather.7.cloned.1.call-update) | async-done | bytes 8388624 | tf_op jit(solution)/shard_map/all_gather | solution.py:97
  263.4 4.1 %multiply_reduce_fusion = f32[4,128,128]{2,1,0:T(8,128)S(1)} fusion(f32[4,32,128,128]{3,2,0,1:T(8,128)} %bitcast.111, f32[4,32]{0,1:T(8,128)S(1)} %get-tuple-element.22), kind=kLoop, calls=%fused_computation | loop fusion | flops 4128768 | bytes 8651264 | tf_op jit(solution)/shard_map/ul,ulec->lec/dot_general | solution.py:28
  267.6 0.7 fusion.12
  268.3 1.0 copy.57
  269.3 0.6 fusion.11
  269.9 1.0 copy.56
  (21 shorter events, 0.1 us)
Async XLA Ops:
  7.2 2.2 copy-start
  7.2 5.6 %copy-start.8 = (bf16[512,512]{1,0:T(8,128)(2,1)S(1)}, bf16[512,512]{1,0:T(8,128)(2,1)}, u32[]{:S(2)}) copy-start(bf16[512,512]{1,0:T(8,128)(2,1)} %param.7) | copy-start | bytes 1572868
  7.2 113.1 %all-gather.5.cloned.1.call-start = ((), (), s32[]{:S(2)}) async-start(), calls=%async_computation | async-start | bytes 8650752 | tf_op jit(solution)/shard_map/all_gather | solution.py:58
  9.3 1.7 copy-start.7
  10.8 252.7 %all-gather.7.cloned.1.call-start = ((), (), s32[]{:S(2)}) async-start(), calls=%async_computation.1 | async-start | bytes 8650752 | tf_op jit(solution)/shard_map/all_gather | solution.py:97
  12.6 1.6 copy-start.11
  12.7 1.5 copy-start.10
  14.2 1.4 copy-start.1
  132.3 1.1 copy-start.13
  133.4 30.4 %copy-start.12 = (pred[512,512]{1,0:T(8,128)(4,1)S(1)}, pred[512,512]{1,0:T(8,128)(4,1)}, u32[]{:S(2)}) copy-start(pred[512,512]{1,0:T(8,128)(4,1)} %copy-done.11) | copy-start | bytes 786436
  162.4 1.4 copy-start.5
  166.4 1.3 copy-start.3
  167.8 6.5 %copy-start.2 = (bf16[4,512,512]{2,1,0:T(8,128)(2,1)S(1)}, bf16[4,512,512]{2,1,0:T(8,128)(2,1)}, u32[]{:S(2)}) copy-start(bf16[4,512,512]{2,1,0:T(8,128)(2,1)} %copy-done.1) | copy-start | bytes 6291460
  174.3 2.7 copy-start.4
  263.4 4.1 %copy-start.6 = (f32[512,4,128]{0,2,1:T(8,128)S(1)}, f32[512,4,128]{0,2,1:T(8,128)}, u32[]{:S(2)}) copy-start(f32[512,4,128]{0,2,1:T(8,128)} %convolution_bitcast_fusion.1) | copy-start | bytes 3145732
  263.4 4.2 %copy-start.9 = (bf16[512,512]{1,0:T(8,128)(2,1)S(1)}, bf16[512,512]{1,0:T(8,128)(2,1)}, u32[]{:S(2)}) copy-start(bf16[512,512]{1,0:T(8,128)(2,1)} %param.7) | copy-start | bytes 1572868
Sparse Core Ops, SparseCore 0:
  11.8 108.5 all-gather.4
  164.0 99.4 all-gather.6
where the time goes:
time: 278 us
  waiting for transfers between devices  190 us (68%)
  matrix products  29.2 us (11%)
  blocking collectives  25.3 us (9%)
  between operations  14.3 us (5%)
  local copies, waits for them, and re-layouts  9.95 us (4%)
  other arithmetic  8.97 us (3%)
    all_gather x1, waiting for transfers between devices, local(): lax.all_gather(running_state[None], 'ctx', axis=0, tiled=True)  104 us
    all_gather x1, waiting for transfers between devices, local(): lax.all_gather(grad_state[None], 'ctx', axis=0, tiled=True)  86 us
    psum x1, blocking collectives, local(): lax.psum((jnp.sum(attended_output * attended_output, axis=1), jnp.sum(sca...  25.3 us
    dot_general x1, matrix products, folder(): jnp.einsum('ul,ulec->lec', scale_factor, block_piece, precision=lax.Preci...  12 us
    unnamed x31, local copies, waits for them, and re-layouts  6.82 us
  transfers between devices with their start and end apart: 2, of which 2 were waited for; matrix products, arithmetic and copies ran while one was open for 6% of the time, Pallas kernels for 0%

commit v1 on v0

v1 whole, which is shorter than its diff:
```python
import functools

import jax
import jax.numpy as jnp
from jax import lax
from jax.experimental import pallas as pl
from jax.experimental.pallas import tpu as pltpu
from jax.sharding import Mesh, PartitionSpec as P

DH = 128
TILE = 128
F32 = jnp.float32
BF16 = jnp.bfloat16
NT = (((1,), (1,)), ((), ()))
TN = (((0,), (0,)), ((), ()))
NN = (((1,), (0,)), ((), ()))
VMEM = pl.BlockSpec(memory_space=pltpu.VMEM)
SMEM = pl.BlockSpec(memory_space=pltpu.SMEM)
PARAMS = pltpu.CompilerParams(vmem_limit_bytes=32 * 2**20)


def dot(left, right, dims):
    return lax.dot_general(left, right, dims, preferred_element_type=F32)


def halves(value):
    high = value.astype(BF16)
    return high, (value - high.astype(F32)).astype(BF16)


def dot_wide(left, right, dims):
    high, low = halves(right)
    return dot(left, high, dims) + dot(left, low, dims)


def rows(count):
    return lax.broadcasted_iota(jnp.int32, (count, DH), 0).astype(F32)


def band(rate, count):
    row = lax.broadcasted_iota(jnp.int32, (TILE, count), 0) + (count - TILE)
    diff = (row - lax.broadcasted_iota(jnp.int32, (TILE, count), 1)).astype(F32)
    return jnp.where(diff >= 0, jnp.exp(-rate * jnp.maximum(diff, 0.0)), 0.0)


def head(h):
    return slice(h * DH, (h + 1) * DH)


def state_kernel(rate_ref, k_ref, v_ref, out_ref):
    count = k_ref.shape[0]
    for h in range(rate_ref.shape[0]):
        weight = jnp.exp(-rate_ref[h] * (count - 1.0 - rows(count)))
        out_ref[head(h), :] = dot_wide(
            k_ref[:, head(h)], v_ref[:, head(h)].astype(F32) * weight, TN
        )


def scan_kernel(reverse, decay_ref, in_ref, out_ref):
    blocks = in_ref.shape[0]
    decay = decay_ref[0]
    total = jnp.zeros(in_ref.shape[1:], F32)
    order = range(blocks - 1, -1, -1) if reverse else range(blocks)
    for b in order:
        out_ref[b] = total
        total = total * decay + in_ref[b]


def inner_kernel(rate_ref, q_ref, k_ref, v_ref, out_ref):
    count = k_ref.shape[0]
    for h in range(rate_ref.shape[0]):
        table = band(rate_ref[h], count)
        for a in range(count // TILE):
            here = slice(a * TILE, (a + 1) * TILE)
            seen = (a + 1) * TILE
            scores = dot(q_ref[here, head(h)], k_ref[:seen, head(h)], NT)
            weights = (scores * table[:, count - seen :]).astype(BF16)
            out_ref[here, head(h)] = dot(weights, v_ref[:seen, head(h)], NN)


def attend_kernel(rate_ref, q_ref, g_ref, gain_ref, inner_ref, prefix_ref, att_ref, sums_ref):
    count = q_ref.shape[0]
    squares = jnp.zeros((count, DH), F32)
    crossing = jnp.zeros((count, DH), F32)
    for h in range(rate_ref.shape[0]):
        weight = jnp.exp(-rate_ref[h] * (rows(count) + 1.0))
        attended = (
            inner_ref[:, head(h)]
            + dot_wide(q_ref[:, head(h)], prefix_ref[head(h), :], NN) * weight
        )
        att_ref[:, head(h)] = attended
        scaled = g_ref[:, head(h)].astype(F32) * gain_ref[:, head(h)]
        squares += attended * attended
        crossing += scaled * attended
    ones = jnp.ones((8, DH), BF16)
    for index, part in enumerate((squares, crossing)):
        high, low = halves(part)
        sums_ref[index : index + 1, :] = (dot(ones, high, NT) + dot(ones, low, NT))[:1]


def norm_kernel(
    total, rate_ref, q_ref, g_ref, gain_ref, att_ref, sums_ref, grad_ref, state_ref, normed_ref
):
    count = q_ref.shape[0]
    ones = jnp.ones((sums_ref.shape[0], DH), F32)

    def spread(index):
        return lax.dot_general(
            sums_ref[:, index, :], ones, TN, precision=lax.Precision.HIGHEST,
            preferred_element_type=F32,
        )

    rinv = lax.rsqrt(spread(0) / total + 1e-06)
    cross = spread(1) / total
    factor = rinv * rinv * rinv * cross
    for h in range(rate_ref.shape[0]):
        weight = jnp.exp(-rate_ref[h] * rows(count))
        attended = att_ref[:, head(h)]
        gain = gain_ref[:, head(h)]
        scaled = g_ref[:, head(h)].astype(F32) * gain
        grad = (rinv * scaled - attended * factor).astype(BF16)
        grad_ref[:, head(h)] = grad
        normed_ref[:, head(h)] = (attended * rinv * gain).astype(BF16)
        state_ref[head(h), :] = dot_wide(q_ref[:, head(h)], grad.astype(F32) * weight, TN)


def back_kernel(
    rate_ref, q_ref, k_ref, v_ref, d_ref, prefix_ref, dq_ref, dk_ref, dv_ref
):
    count = q_ref.shape[0]
    for h in range(rate_ref.shape[0]):
        table = band(rate_ref[h], count)
        weight = jnp.exp(-rate_ref[h] * (rows(count) + 1.0))
        past = dot_wide(d_ref[:, head(h)], prefix_ref[head(h), :], NT) * weight
        for a in range(count // TILE):
            here = slice(a * TILE, (a + 1) * TILE)
            seen = (a + 1) * TILE
            part = table[:, count - seen :]
            q, d = q_ref[here, head(h)], d_ref[here, head(h)]
            weights = (dot(q, k_ref[:seen, head(h)], NT) * part).astype(BF16)
            grads = (dot(d, v_ref[:seen, head(h)], NT) * part).astype(BF16)
            dq_ref[here, head(h)] = (
                dot(grads, k_ref[:seen, head(h)], NN) + past[here, :]
            ).astype(BF16)
            dk, dv = dot(grads, q, TN), dot(weights, d, TN)
            if a:
                before = slice(0, a * TILE)
                dk_ref[before, head(h)] += dk[before, :]
                dv_ref[before, head(h)] += dv[before, :]
            dk_ref[here, head(h)] = dk[here, :]
            dv_ref[here, head(h)] = dv[here, :]


def final_kernel(rate_ref, k_ref, v_ref, suffix_ref, dk_ref, dv_ref, kout_ref, vout_ref):
    count = k_ref.shape[0]
    for h in range(rate_ref.shape[0]):
        weight = jnp.exp(-rate_ref[h] * (count - rows(count)))
        suffix = suffix_ref[head(h), :]
        kout_ref[:, head(h)] = (
            dk_ref[:, head(h)] + dot_wide(v_ref[:, head(h)], suffix, NT) * weight
        ).astype(BF16)
        vout_ref[:, head(h)] = (
            dv_ref[:, head(h)] + dot_wide(k_ref[:, head(h)], suffix, NN) * weight
        ).astype(BF16)


def call(kernel, shapes, specs, *args, name, flops=0, size=0):
    return pl.pallas_call(
        kernel,
        out_shape=shapes,
        in_specs=specs,
        out_specs=jax.tree.map(lambda _: VMEM, shapes),
        compiler_params=PARAMS,
        cost_estimate=pl.CostEstimate(flops=flops, bytes_accessed=size, transcendentals=0),
        name=name,
    )(*args)


def scan(state, decay, reverse):
    axes = ("y", "x")
    blocks = lax.axis_size(axes)
    pieces = state.reshape(blocks, -1, DH)
    mine = lax.all_to_all(pieces, axes, 0, 0, tiled=True)
    owner = lax.axis_index(axes) * decay.shape[0] // blocks
    rate = lax.dynamic_slice(decay, (owner,), (1,))
    sums = call(
        functools.partial(scan_kernel, reverse),
        jax.ShapeDtypeStruct(mine.shape, F32),
        [SMEM, VMEM],
        rate, mine,
        name="scan",
        size=2 * mine.size * 4,
    )
    return lax.all_to_all(sums, axes, 0, 0, tiled=True).reshape(state.shape)


def local(queries, keys, values, out_grad, decay_rate, gain):
    count, width = queries.shape
    heads = decay_rate.shape[0]
    shape = jax.ShapeDtypeStruct
    gain = gain[None, :]
    decay = jnp.exp(-decay_rate * count)
    pair = 2 * count * count * DH * heads
    wide = 2 * count * DH * DH * heads * 2
    state = call(
        state_kernel, shape((width, DH), F32), [SMEM, VMEM, VMEM],
        decay_rate, keys, values, name="state", flops=wide, size=4 * count * width,
    )
    prefix = scan(state, decay, False)
    inner = call(
        inner_kernel, shape((count, width), F32), [SMEM] + [VMEM] * 3,
        decay_rate, queries, keys, values, name="inner", flops=2 * pair, size=10 * count * width,
    )
    attended, sums = call(
        attend_kernel,
        (shape((count, width), F32), shape((2, count), F32)),
        [SMEM] + [VMEM] * 5,
        decay_rate, queries, out_grad, gain, inner, prefix,
        name="attend", flops=wide, size=12 * count * width,
    )
    sums = lax.all_gather(sums[None], ("z", "c"), axis=0, tiled=True)
    total = float(heads * lax.axis_size(("z", "c")) * DH)
    grad, state, normed = call(
        functools.partial(norm_kernel, total),
        (shape((count, width), BF16), shape((width, DH), F32), shape((count, width), BF16)),
        [SMEM] + [VMEM] * 5,
        decay_rate, queries, out_grad, gain, attended, sums,
        name="norm", flops=wide, size=12 * count * width,
    )
    suffix = scan(state, decay, True)
    dq, dk, dv = call(
        back_kernel,
        (shape((count, width), BF16), shape((count, width), F32), shape((count, width), F32)),
        [SMEM] + [VMEM] * 5,
        decay_rate, queries, keys, values, grad, prefix,
        name="back", flops=5 * pair, size=18 * count * width,
    )
    dk, dv = call(
        final_kernel,
        (shape((count, width), BF16), shape((count, width), BF16)),
        [SMEM] + [VMEM] * 5,
        decay_rate, keys, values, suffix, dk, dv,
        name="final", flops=2 * wide, size=16 * count * width,
    )
    return normed, dq, dk, dv


def solution(mesh):
    fine = Mesh(mesh.devices.reshape(8, 4, 8, 2), ("y", "x", "z", "c"))
    ctx, head_axes = ("y", "x"), ("z", "c")
    tokens = P(ctx, head_axes)
    return jax.shard_map(
        local,
        mesh=fine,
        in_specs=(tokens,) * 4 + (P(head_axes),) * 2,
        out_specs=(tokens,) * 4,
        check_vma=False,
    )
```

time: 278 us -> 111 us (0.40)
  waiting for transfers between devices: 190 us -> 20.3 us
  matrix products: 29.2 us -> 0 us
  starting transfers between devices: 0.08 us -> 19.8 us
  Pallas kernels: 0 us -> 19.3 us
  blocking collectives: 25.3 us -> 41.8 us
  between operations: 14.3 us -> 0.76 us
  other arithmetic: 8.97 us -> 0.01 us
    all_gather x2 -> x0, waiting for transfers between devices: 190 us -> none  [the longest x1 104 us: local(): lax.all_gather(running_state[None], 'ctx', axis=0, tiled=True)]
    dot_general x13 -> x0, matrix products: 29.2 us -> none  [the longest x1 12 us: folder(): jnp.einsum('ul,ulec->lec', scale_factor, block_piece, precision=lax.Preci...]
    all_gather x0 -> x1, blocking collectives: none -> 26.9 us  [local(): sums = lax.all_gather(sums[None], ('z', 'c'), axis=0, tiled=True)]
    psum x1 -> x0, blocking collectives: 25.3 us -> none  [local(): lax.psum((jnp.sum(attended_output * attended_output, axis=1), jnp.sum(sca...]
    all_to_all x0 -> x3, waiting for transfers between devices: none -> 20.3 us  [the longest x2 10.4 us: scan(): return lax.all_to_all(sums, axes, 0, 0, tiled=True).reshape(state.shape)]
    all_to_all x0 -> x3, starting transfers between devices: none -> 19.8 us  [the longest x1 10.6 us: scan(): mine = lax.all_to_all(pieces, axes, 0, 0, tiled=True)]
    pallas_call x0 -> x8, Pallas kernels: none -> 19.3 us  [call(): pl.pallas_call(kernel, out_shape=shapes, in_specs=specs, out_specs=jax.tr...]
    all_to_all x0 -> x1, blocking collectives: none -> 14.9 us  [scan(): mine = lax.all_to_all(pieces, axes, 0, 0, tiled=True)]
  transfers between devices with their start and end apart: 2 -> 3, of which waited for: 2 -> 3; matrix products, arithmetic and copies ran while one was open for 6% -> 1% of each run, Pallas kernels for 0% -> 8%
where the time goes in v1:
time: 111 us; the launch traced here: 109 us
  blocking collectives  41.8 us (38%)
  waiting for transfers between devices  20.3 us (18%)
  starting transfers between devices  19.8 us (18%)
  Pallas kernels  19.3 us (17%)
  local copies, waits for them, and re-layouts  7.26 us (7%)
    all_gather x1, blocking collectives, local(): sums = lax.all_gather(sums[None], ('z', 'c'), axis=0, tiled=True)  26.9 us
    pallas_call x8, Pallas kernels, call(): pl.pallas_call(kernel, out_shape=shapes, in_specs=specs, out_specs=jax.tr...  19.3 us
    all_to_all x1, blocking collectives, scan(): mine = lax.all_to_all(pieces, axes, 0, 0, tiled=True)  14.9 us
    all_to_all x1, starting transfers between devices, scan(): mine = lax.all_to_all(pieces, axes, 0, 0, tiled=True)  10.6 us
    all_to_all x2, waiting for transfers between devices, scan(): return lax.all_to_all(sums, axes, 0, 0, tiled=True).reshape(state.shape)  10.4 us
    all_to_all x1, waiting for transfers between devices, scan(): mine = lax.all_to_all(pieces, axes, 0, 0, tiled=True)  9.91 us
    all_to_all x2, starting transfers between devices, scan(): return lax.all_to_all(sums, axes, 0, 0, tiled=True).reshape(state.shape)  9.12 us
    unnamed x26, local copies, waits for them, and re-layouts  6.67 us
  transfers between devices with their start and end apart: 3, of which 3 were waited for; matrix products, arithmetic and copies ran while one was open for 1% of the time, Pallas kernels for 8%

profile of v1, /device:TPU:1, one launch (start us, length us, event | category | flops | bytes accessed | tf_op | source)
XLA Modules:
  0.0 109.2 jit_solution(2811026929084702656)
XLA Ops:
  0.6 0.0 copy-start
  0.6 1.0 copy-done
  1.7 0.0 copy-start.2
  1.7 1.0 copy-done.2
  2.7 0.0 copy-start.8
  2.7 0.7 copy-done.8
  3.4 1.8 %state.1 = f32[512,128]{1,0:T(8,128)} custom-call(f32[4]{0:T(128)S(1)} %copy-done.8, bf16[512,512]{1,0:T(8,128)(2,1)S(1)} %copy-done, bf16[512,512]{1,0:T(8,128)(2,1)S(1)} %copy-done.2), custom_call_target="tpu_custom_call" | custom-call | flops 134217728 | bytes 1048576 | tf_op jit(solution)/shard_map/state/pallas_call | solution.py:168
  5.2 0.0 copy-start.4
  5.2 10.6 %all-to-all-start = ((f32[32,16,128]{2,1,0:T(8,128)}), f32[32,16,128]{2,1,0:T(8,128)S(1)}, u32[]{:S(2)}, u32[]{:S(2)}) async-start(f32[32,16,128]{2,1,0:T(8,128)} %bitcast.1), calls=%async_computation | async-start | bytes 524288 | tf_op jit(solution)/shard_map/all_to_all | solution.py:183
  15.8 0.0 copy-start.9
  15.9 0.6 copy-done.9
  16.5 0.6 dynamic_slice.4.decay_ref
  17.1 0.0 copy-start.1
  17.1 0.0 copy-start.3
  17.1 9.9 %all-to-all-done.in_ref = f32[32,16,128]{2,1,0:T(8,128)S(1)} async-done(((f32[32,16,128]{2,1,0:T(8,128)}), f32[32,16,128]{2,1,0:T(8,128)S(1)}, u32[]{:S(2)}, u32[]{:S(2)}) %all-to-all-start) | async-done | bytes 262176 | tf_op jit(solution)/shard_map/all_to_all | solution.py:183
  27.0 1.4 %scan.2 = f32[32,16,128]{2,1,0:T(8,128)} custom-call(f32[1]{0:T(128)} %dynamic_slice.4.decay_ref, f32[32,16,128]{2,1,0:T(8,128)S(1)} %all-to-all-done.in_ref), custom_call_target="tpu_custom_call" | custom-call | bytes 524288 | tf_op jit(solution)/shard_map/scan/pallas_call | solution.py:168
  28.4 4.8 %all-to-all-start.1 = ((f32[32,16,128]{2,1,0:T(8,128)}), f32[32,16,128]{2,1,0:T(8,128)S(1)}, u32[]{:S(2)}, u32[]{:S(2)}) async-start(f32[32,16,128]{2,1,0:T(8,128)} %scan.2), calls=%async_computation.1 | async-start | bytes 524288 | tf_op jit(solution)/shard_map/all_to_all | solution.py:194
  33.2 0.0 copy-done.4
  33.2 0.0 copy-done.1
  33.2 0.0 copy-done.3
  33.2 0.0 copy-start.5
  33.2 2.8 %inner.1.inner_ref = f32[512,512]{1,0:T(8,128)S(1)} custom-call(f32[4]{0:T(128)S(1)} %copy-done.9, bf16[512,512]{1,0:T(8,128)(2,1)S(1)} %copy-done.4, bf16[512,512]{1,0:T(8,128)(2,1)S(1)} %copy-done.1, bf16[512,512]{1,0:T(8,128)(2,1)S(1)} %copy-done.3), custom_call_target="tpu_custom_call" | custom-call | flops 536870912 | bytes 2621440 | tf_op jit(solution)/shard_map/inner/pallas_call | solution.py:168
  36.1 0.0 copy-start.10
  36.1 7.5 %all-to-all-done.1 = f32[32,16,128]{2,1,0:T(8,128)S(1)} async-done(((f32[32,16,128]{2,1,0:T(8,128)}), f32[32,16,128]{2,1,0:T(8,128)S(1)}, u32[]{:S(2)}, u32[]{:S(2)}) %all-to-all-start.1) | async-done | bytes 262176 | tf_op jit(solution)/shard_map/all_to_all | solution.py:194
  43.6 0.0 copy-done.5
  43.6 0.0 copy-done.10
  43.6 1.3 %attend.1 = (f32[512,512]{1,0:T(8,128)S(1)}, f32[2,512]{1,0:T(2,128)S(1)}) custom-call(f32[4]{0:T(128)S(1)} %copy-done.9, bf16[512,512]{1,0:T(8,128)(2,1)S(1)} %copy-done.4, bf16[512,512]{1,0:T(8,128)(2,1)S(1)} %copy-done.5, f32[1,512]{1,0:T(1,128)S(1)} %bitcast.10, f32[512,512]{1,0:T(8,128)S(1)} %inner.1.inner_ref, f32[512,128]{1,0:T(8,128)S(1)} %bitcast.6), custom_call_target="tpu_custom_call" | custom-call | flops 134217728 | bytes 3145728 | tf_op jit(solution)/shard_map/attend/pallas_call | solution.py:168
  44.9 26.9 %all-gather.1.sums_ref = f32[16,2,512]{2,1,0:T(2,128)S(1)} all-gather(f32[1,2,512]{2,1,0:T(2,128)S(1)} %bitcast.12), channel_id=2, replica_groups=mesh['y'=8,'x'=4,'z'=8,'c'=2] {'z','c'}, dimensions={0}, use_global_device_ids=true | all-gather | bytes 69632 | tf_op jit(solution)/shard_map/all_gather | solution.py:221
  71.9 2.7 %norm.1 = (bf16[512,512]{1,0:T(8,128)(2,1)S(1)}, f32[512,128]{1,0:T(8,128)S(1)}, bf16[512,512]{1,0:T(8,128)(2,1)}) custom-call(f32[4]{0:T(128)S(1)} %copy-done.9, bf16[512,512]{1,0:T(8,128)(2,1)S(1)} %copy-done.4, bf16[512,512]{1,0:T(8,128)(2,1)S(1)} %copy-done.5, f32[1,512]{1,0:T(1,128)S(1)} %bitcast.11, f32[512,512]{1,0:T(8,128)S(1)} %get-tuple-element.14.att_ref, ...), custom_call_target="tpu_custom_call" | custom-call | flops 134217728 | bytes 3145728 | tf_op jit(solution)/shard_map/norm/pallas_call | solution.py:168
  74.5 0.0 copy-start.11
  74.5 14.9 %all_to_all.20.in_ref = f32[32,16,128]{2,1,0:T(8,128)S(1)} all-to-all(f32[32,16,128]{2,1,0:T(8,128)S(1)} %bitcast.9), channel_id=1, replica_groups=mesh['y'=8,'x'=4,'z'=8,'c'=2] {'y','x'}, dimensions={0} | all-to-all | bytes 524288 | tf_op jit(solution)/shard_map/all_to_all | solution.py:183
  89.5 1.4 %scan.3 = f32[32,16,128]{2,1,0:T(8,128)} custom-call(f32[1]{0:T(128)} %dynamic_slice.4.decay_ref, f32[32,16,128]{2,1,0:T(8,128)S(1)} %all_to_all.20.in_ref), custom_call_target="tpu_custom_call" | custom-call | bytes 524288 | tf_op jit(solution)/shard_map/scan/pallas_call | solution.py:168
  90.9 0.0 copy-done.11
  90.9 4.4 %all-to-all-start.3 = ((f32[32,16,128]{2,1,0:T(8,128)}), f32[32,16,128]{2,1,0:T(8,128)S(1)}, u32[]{:S(2)}, u32[]{:S(2)}) async-start(f32[32,16,128]{2,1,0:T(8,128)} %scan.3), calls=%async_computation.3 | async-start | bytes 524288 | tf_op jit(solution)/shard_map/all_to_all | solution.py:194
  95.2 0.0 copy-start.12
  95.2 1.0 copy-done.12
  96.3 5.5 %back.1 = (bf16[512,512]{1,0:T(8,128)(2,1)}, f32[512,512]{1,0:T(8,128)S(1)}, f32[512,512]{1,0:T(8,128)S(1)}) custom-call(f32[4]{0:T(128)S(1)} %copy-done.9, bf16[512,512]{1,0:T(8,128)(2,1)S(1)} %copy-done.4, bf16[512,512]{1,0:T(8,128)(2,1)S(1)} %copy-done.1, bf16[512,512]{1,0:T(8,128)(2,1)S(1)} %copy-done.3, bf16[512,512]{1,0:T(8,128)(2,1)S(1)} %copy-done.12, ...), custom_call_target="tpu_custom_call" | custom-call | flops 1342177280 | bytes 4718592 | tf_op jit(solution)/shard_map/back/pallas_call | solution.py:168
  101.8 0.0 copy-start.6
  101.8 1.0 copy-done.6
  102.8 2.9 %all-to-all-done.3 = f32[32,16,128]{2,1,0:T(8,128)S(1)} async-done(((f32[32,16,128]{2,1,0:T(8,128)}), f32[32,16,128]{2,1,0:T(8,128)S(1)}, u32[]{:S(2)}, u32[]{:S(2)}) %all-to-all-start.3) | async-done | bytes 262176 | tf_op jit(solution)/shard_map/all_to_all | solution.py:194
  105.7 0.0 copy-start.7
  105.7 1.2 %copy-done.7 = f32[512,512]{1,0:T(8,128)S(1)} copy-done((f32[512,512]{1,0:T(8,128)S(1)}, f32[512,512]{1,0:T(8,128)}, u32[]{:S(2)}) %copy-start.7) | copy-done | bytes 1048600
  106.9 2.3 %final.1 = (bf16[512,512]{1,0:T(8,128)(2,1)}, bf16[512,512]{1,0:T(8,128)(2,1)}) custom-call(f32[4]{0:T(128)S(1)} %copy-done.9, bf16[512,512]{1,0:T(8,128)(2,1)S(1)} %copy-done.1, bf16[512,512]{1,0:T(8,128)(2,1)S(1)} %copy-done.3, f32[512,128]{1,0:T(8,128)S(1)} %bitcast.8, f32[512,512]{1,0:T(8,128)S(1)} %get-tuple-element.20.dk_ref, f32[512,512]{1,0:T(8,128)S(1)} %copy-done.7), custom_call_target="tpu_custom_call" | custom-call | flops 268435456 | bytes 4194304 | tf_op jit(solution)/shard_map/final/pallas_call | solution.py:168
  (1 shorter events, 0.0 us)
Async XLA Ops:
  0.6 1.0 copy-start
  1.7 1.0 copy-start.2
  2.7 0.7 copy-start.8
  5.2 28.0 %copy-start.4 = (bf16[512,512]{1,0:T(8,128)(2,1)S(1)}, bf16[512,512]{1,0:T(8,128)(2,1)}, u32[]{:S(2)}) copy-start(bf16[512,512]{1,0:T(8,128)(2,1)} %q_ref.7) | copy-start | bytes 1572868
  5.2 21.8 %all-to-all-start = ((f32[32,16,128]{2,1,0:T(8,128)}), f32[32,16,128]{2,1,0:T(8,128)S(1)}, u32[]{:S(2)}, u32[]{:S(2)}) async-start(f32[32,16,128]{2,1,0:T(8,128)} %bitcast.1), calls=%async_computation | async-start | bytes 524288 | tf_op jit(solution)/shard_map/all_to_all | solution.py:183
  15.8 0.7 copy-start.9
  17.1 16.1 %copy-start.1 = (bf16[512,512]{1,0:T(8,128)(2,1)S(1)}, bf16[512,512]{1,0:T(8,128)(2,1)}, u32[]{:S(2)}) copy-start(bf16[512,512]{1,0:T(8,128)(2,1)} %k_ref.7) | copy-start | bytes 1572868
  17.1 16.1 %copy-start.3 = (bf16[512,512]{1,0:T(8,128)(2,1)S(1)}, bf16[512,512]{1,0:T(8,128)(2,1)}, u32[]{:S(2)}) copy-start(bf16[512,512]{1,0:T(8,128)(2,1)} %v_ref.7) | copy-start | bytes 1572868
  28.4 15.2 %all-to-all-start.1 = ((f32[32,16,128]{2,1,0:T(8,128)}), f32[32,16,128]{2,1,0:T(8,128)S(1)}, u32[]{:S(2)}, u32[]{:S(2)}) async-start(f32[32,16,128]{2,1,0:T(8,128)} %scan.2), calls=%async_computation.1 | async-start | bytes 524288 | tf_op jit(solution)/shard_map/all_to_all | solution.py:194
  33.2 10.4 %copy-start.5 = (bf16[512,512]{1,0:T(8,128)(2,1)S(1)}, bf16[512,512]{1,0:T(8,128)(2,1)}, u32[]{:S(2)}) copy-start(bf16[512,512]{1,0:T(8,128)(2,1)} %g_ref.3) | copy-start | bytes 1572868
  36.1 7.5 %copy-start.10 = (f32[512]{0:T(512)S(1)}, f32[512]{0:T(512)}, u32[]{:S(2)}) copy-start(f32[512]{0:T(512)} %param.11) | copy-start | bytes 6148
  74.5 16.3 %copy-start.11 = (bf16[512,512]{1,0:T(8,128)(2,1)}, bf16[512,512]{1,0:T(8,128)(2,1)S(1)}, u32[]{:S(2)}) copy-start(bf16[512,512]{1,0:T(8,128)(2,1)S(1)} %get-tuple-element.17.d_ref) | copy-start | bytes 1572868
  90.9 14.8 %all-to-all-start.3 = ((f32[32,16,128]{2,1,0:T(8,128)}), f32[32,16,128]{2,1,0:T(8,128)S(1)}, u32[]{:S(2)}, u32[]{:S(2)}) async-start(f32[32,16,128]{2,1,0:T(8,128)} %scan.3), calls=%async_computation.3 | async-start | bytes 524288 | tf_op jit(solution)/shard_map/all_to_all | solution.py:194
  95.2 1.0 copy-start.12
  101.8 1.0 copy-start.6
  105.7 1.2 %copy-start.7 = (f32[512,512]{1,0:T(8,128)S(1)}, f32[512,512]{1,0:T(8,128)}, u32[]{:S(2)}) copy-start(f32[512,512]{1,0:T(8,128)} %copy-done.6) | copy-start | bytes 3145732

commit v2 on v1

v2 whole, which is shorter than its diff:
```python
import functools

import jax
import jax.numpy as jnp
from jax import lax
from jax.experimental import pallas as pl
from jax.experimental.pallas import tpu as pltpu
from jax.sharding import Mesh, PartitionSpec as P

DH = 128
TILE = 128
F32 = jnp.float32
BF16 = jnp.bfloat16
NT = (((1,), (1,)), ((), ()))
TN = (((0,), (0,)), ((), ()))
NN = (((1,), (0,)), ((), ()))
VMEM = pl.BlockSpec(memory_space=pltpu.VMEM)
SMEM = pl.BlockSpec(memory_space=pltpu.SMEM)
ANY = pl.BlockSpec(memory_space=pl.ANY)


def dot(left, right, dims):
    return lax.dot_general(left, right, dims, preferred_element_type=F32)


def halves(value):
    high = value.astype(BF16)
    return high, (value - high.astype(F32)).astype(BF16)


def dot_wide(left, right):
    return dot(
        jnp.concatenate([left, left], axis=1), jnp.concatenate(halves(right), axis=0), NN
    )


def rows(count):
    return lax.broadcasted_iota(jnp.int32, (count, DH), 0).astype(F32)


def band(rate, count):
    row = lax.broadcasted_iota(jnp.int32, (TILE, count), 0) + (count - TILE)
    diff = (row - lax.broadcasted_iota(jnp.int32, (TILE, count), 1)).astype(F32)
    return jnp.where(diff >= 0, jnp.exp(-rate * jnp.maximum(diff, 0.0)), 0.0)


def head(h):
    return slice(h * DH, (h + 1) * DH)


def diagonal():
    return lax.broadcasted_iota(jnp.int32, (TILE, TILE), 0) == lax.broadcasted_iota(
        jnp.int32, (TILE, TILE), 1
    )


def to_rows(part):
    sums = jnp.sum(part, axis=1, keepdims=True)
    mask = diagonal()
    return [
        jnp.sum(jnp.where(mask, sums[a * TILE : (a + 1) * TILE, :], 0.0), axis=0, keepdims=True)
        for a in range(part.shape[0] // TILE)
    ]


def to_columns(table, first, tiles):
    mask = diagonal()
    return jnp.concatenate(
        [
            jnp.sum(jnp.where(mask, table[a : a + 1, :], 0.0), axis=1, keepdims=True)
            for a in range(first, first + tiles)
        ],
        axis=0,
    )


def state_kernel(rate_hbm, k_hbm, v_hbm, out_ref, rate_ref, k_ref, v_ref, sems):
    count = k_ref.shape[0]
    copies = [
        pltpu.make_async_copy(rate_hbm, rate_ref, sems.at[0]),
        pltpu.make_async_copy(k_hbm, k_ref, sems.at[1]),
        pltpu.make_async_copy(v_hbm, v_ref, sems.at[2]),
    ]
    for copy in copies:
        copy.start()
    back = count - 1.0 - rows(count)
    for copy in copies:
        copy.wait()
    for h in range(rate_ref.shape[0]):
        weight = jnp.exp(-rate_ref[h] * back)
        both = jnp.concatenate(halves(v_ref[:, head(h)].astype(F32) * weight), axis=1)
        sums = dot(k_ref[:, head(h)], both, TN)
        out_ref[head(h), :] = sums[:, :DH] + sums[:, DH:]


def scan_kernel(reverse, decay_ref, in_ref, out_ref):
    blocks = in_ref.shape[0]
    decay = decay_ref[...]
    total = jnp.zeros(in_ref.shape[1:], F32)
    order = range(blocks - 1, -1, -1) if reverse else range(blocks)
    for b in order:
        out_ref[b] = total
        total = total * decay + in_ref[b]


def inner_kernel(rate_ref, q_ref, k_ref, v_ref, out_ref, start_ref, turned_ref):
    count = k_ref.shape[0]
    for h in range(rate_ref.shape[0]):
        rate = rate_ref[h]
        table = band(rate, count)
        start_ref[:, head(h)] = jnp.exp(-rate * (rows(count) + 1.0))
        scaled = q_ref[:, head(h)].astype(F32) * jnp.exp(-rate * rows(count))
        high, low = halves(scaled.T)
        turned_ref[2 * h * DH : (2 * h + 1) * DH, :] = high
        turned_ref[(2 * h + 1) * DH : (2 * h + 2) * DH, :] = low
        for a in range(count // TILE):
            here = slice(a * TILE, (a + 1) * TILE)
            seen = (a + 1) * TILE
            scores = dot(q_ref[here, head(h)], k_ref[:seen, head(h)], NT)
            weights = (scores * table[:, count - seen :]).astype(BF16)
            out_ref[here, head(h)] = dot(weights, v_ref[:seen, head(h)], NN)


def attend_kernel(q_ref, g_ref, gain_ref, inner_ref, start_ref, prefix_ref, att_ref, sums_ref):
    count, width = q_ref.shape
    squares = jnp.zeros((count, DH), F32)
    crossing = jnp.zeros((count, DH), F32)
    for h in range(width // DH):
        attended = (
            inner_ref[:, head(h)]
            + dot_wide(q_ref[:, head(h)], prefix_ref[head(h), :]) * start_ref[:, head(h)]
        )
        att_ref[:, head(h)] = attended
        scaled = g_ref[:, head(h)].astype(F32) * gain_ref[:, head(h)]
        squares += attended * attended
        crossing += scaled * attended
    both = jnp.concatenate(to_rows(squares) + to_rows(crossing), axis=0)
    for j in range(sums_ref.shape[0]):
        sums_ref[j] = both


def norm_scales(total, sums_ref):
    tiles = sums_ref.shape[1] // 2
    table = jnp.sum(sums_ref[...], axis=0) / total
    rinv = lax.rsqrt(table[:tiles, :] + 1e-06)
    factor = rinv * rinv * rinv * table[tiles:, :]
    return rinv, factor, tiles


def norm_kernel(total, g_ref, gain_ref, att_ref, turned_ref, sums_ref, grad_ref, state_ref):
    rinv, factor, tiles = norm_scales(total, sums_ref)
    rinv, factor = to_columns(rinv, 0, tiles), to_columns(factor, 0, tiles)
    for h in range(g_ref.shape[1] // DH):
        scaled = g_ref[:, head(h)].astype(F32) * gain_ref[:, head(h)]
        grad = (rinv * scaled - att_ref[:, head(h)] * factor).astype(BF16)
        grad_ref[:, head(h)] = grad
        sums = dot(turned_ref[2 * h * DH : (2 * h + 2) * DH, :], grad, NN)
        state_ref[head(h), :] = sums[:DH, :] + sums[DH:, :]


def back_kernel(
    total, rate_ref, q_ref, k_ref, v_ref, d_ref, prefix_ref, start_ref, att_ref, gain_ref, sums_ref,
    normed_ref, dq_ref, dk_ref, dv_ref, tail_ref,
):
    count = q_ref.shape[0]
    rinv, _, tiles = norm_scales(total, sums_ref)
    rinv = to_columns(rinv, 0, tiles)
    for h in range(rate_ref.shape[0]):
        normed_ref[:, head(h)] = (att_ref[:, head(h)] * rinv * gain_ref[:, head(h)]).astype(BF16)
        table = band(rate_ref[h], count)
        tail_ref[:, head(h)] = jnp.exp(-rate_ref[h] * (count - rows(count)))
        past = dot_wide(d_ref[:, head(h)], prefix_ref[head(h), :].T) * start_ref[:, head(h)]
        for a in range(count // TILE):
            here = slice(a * TILE, (a + 1) * TILE)
            seen = (a + 1) * TILE
            part = table[:, count - seen :]
            q, d = q_ref[here, head(h)], d_ref[here, head(h)]
            weights = (dot(q, k_ref[:seen, head(h)], NT) * part).astype(BF16)
            grads = (dot(d, v_ref[:seen, head(h)], NT) * part).astype(BF16)
            dq_ref[here, head(h)] = (
                dot(grads, k_ref[:seen, head(h)], NN) + past[here, :]
            ).astype(BF16)
            dk, dv = dot(grads, q, TN), dot(weights, d, TN)
            if a:
                before = slice(0, a * TILE)
                dk_ref[before, head(h)] += dk[before, :]
                dv_ref[before, head(h)] += dv[before, :]
            dk_ref[here, head(h)] = dk[here, :]
            dv_ref[here, head(h)] = dv[here, :]


def final_kernel(
    k_ref, v_ref, suffix_ref, dk_ref, dv_ref, tail_ref, kout_hbm, vout_hbm, kout_ref, vout_ref, sems
):
    heads = k_ref.shape[1] // DH
    copies = []
    for h in range(heads):
        tail = tail_ref[:, head(h)]
        suffix = suffix_ref[head(h), :]
        kout_ref[:, head(h)] = (
            dk_ref[:, head(h)] + dot_wide(v_ref[:, head(h)], suffix.T) * tail
        ).astype(BF16)
        vout_ref[:, head(h)] = (
            dv_ref[:, head(h)] + dot_wide(k_ref[:, head(h)], suffix) * tail
        ).astype(BF16)
        for index, (held, out) in enumerate(((kout_ref, kout_hbm), (vout_ref, vout_hbm))):
            copy = pltpu.make_async_copy(
                held.at[:, head(h)], out.at[:, head(h)], sems.at[2 * h + index]
            )
            copy.start()
            copies.append(copy)
    for copy in copies:
        copy.wait()


def call(kernel, shapes, specs, *args, name, flops, size, mib=8, out_specs=None, scratch=()):
    return pl.pallas_call(
        kernel,
        out_shape=shapes,
        in_specs=specs,
        out_specs=out_specs or jax.tree.map(lambda _: VMEM, shapes),
        scratch_shapes=scratch,
        compiler_params=pltpu.CompilerParams(vmem_limit_bytes=mib * 2**20),
        cost_estimate=pl.CostEstimate(flops=flops, bytes_accessed=size, transcendentals=0),
        name=name,
    )(*args)


def scan(state, decay, reverse):
    axes = ("y", "x")
    blocks = lax.axis_size(axes)
    pieces = state.reshape(blocks, -1, DH)
    mine = lax.all_to_all(pieces, axes, 0, 0, tiled=True)
    sums = call(
        functools.partial(scan_kernel, reverse),
        jax.ShapeDtypeStruct(mine.shape, F32),
        [VMEM, VMEM],
        decay, mine,
        name="scan", flops=2 * mine.size, size=2 * mine.size * 4, mib=2,
    )
    return lax.all_to_all(sums, axes, 0, 0, tiled=True).reshape(state.shape)


def local(queries, keys, values, out_grad, decay_rate, gain):
    count, width = queries.shape
    heads = decay_rate.shape[0]
    ctx, head_axes = ("y", "x"), ("z", "c")
    shape = jax.ShapeDtypeStruct
    whole32, whole16 = shape((count, width), F32), shape((count, width), BF16)
    state_shape = shape((width, DH), F32)
    gain = gain[None, :]
    owner = lax.axis_index(ctx) * heads // lax.axis_size(ctx)
    decay = jnp.exp(-lax.dynamic_slice(decay_rate, (owner,), (1,)) * count)
    decay = jnp.broadcast_to(decay[None, :], (1, DH))
    pair = 2 * count * count * DH * heads
    wide = 4 * count * DH * DH * heads
    unit = count * width
    state = call(
        state_kernel, state_shape, [ANY] * 3, decay_rate, keys, values,
        name="state", flops=wide, size=4 * unit, mib=48,
        scratch=[
            pltpu.SMEM((heads,), F32),
            pltpu.VMEM((count, width), BF16),
            pltpu.VMEM((count, width), BF16),
            pltpu.SemaphoreType.DMA((3,)),
        ],
    )
    prefix = scan(state, decay, False)
    inner, start, turned = call(
        inner_kernel, (whole32, whole32, shape((2 * width, count), BF16)), [SMEM] + [VMEM] * 3,
        decay_rate, queries, keys, values,
        name="inner", flops=2 * pair, size=18 * unit, mib=12,
    )
    groups = lax.axis_size(head_axes)
    attended, sums = call(
        attend_kernel, (whole32, shape((groups, 2 * count // TILE, TILE), F32)), [VMEM] * 6,
        queries, out_grad, gain, inner, start, prefix,
        name="attend", flops=wide, size=16 * unit,
    )
    sums = lax.all_to_all(sums, head_axes, 0, 0, tiled=True)
    total = float(heads * groups * DH)
    grad, state = call(
        functools.partial(norm_kernel, total), (whole16, state_shape), [VMEM] * 5,
        out_grad, gain, attended, turned, sums,
        name="norm", flops=wide, size=12 * unit,
    )
    suffix = scan(state, decay, True)
    normed, dq, dk, dv, tail = call(
        functools.partial(back_kernel, total), (whole16, whole16, whole32, whole32, whole32),
        [SMEM] + [VMEM] * 9,
        decay_rate, queries, keys, values, grad, prefix, start, attended, gain, sums,
        name="back", flops=5 * pair, size=32 * unit, mib=16,
    )
    dk, dv = call(
        final_kernel, (whole16, whole16), [VMEM] * 6,
        keys, values, suffix, dk, dv, tail,
        name="final", flops=2 * wide, size=20 * unit, out_specs=(ANY, ANY),
        scratch=[
            pltpu.VMEM((count, width), BF16),
            pltpu.VMEM((count, width), BF16),
            pltpu.SemaphoreType.DMA((2 * heads,)),
        ],
    )
    return normed, dq, dk, dv


def solution(mesh):
    fine = Mesh(mesh.devices.reshape(8, 4, 8, 2), ("y", "x", "z", "c"))
    ctx, head_axes = ("y", "x"), ("z", "c")
    tokens = P(ctx, head_axes)
    return jax.shard_map(
        local,
        mesh=fine,
        in_specs=(tokens,) * 4 + (P(head_axes),) * 2,
        out_specs=(tokens,) * 4,
        check_vma=False,
    )
```

time: 111 us -> 106 us (0.955)
  local copies, waits for them, and re-layouts: 7.26 us -> 16.7 us
  waiting for transfers between devices: 20.3 us -> 14.7 us
  blocking collectives: 41.8 us -> 36.6 us
  Pallas kernels: 19.3 us -> 15 us
    all_gather x1 -> x0, blocking collectives: 26.9 us -> none  [local(): sums = lax.all_gather(sums[None], ('z', 'c'), axis=0, tiled=True)]
    all_to_all x0 -> x1, blocking collectives: none -> 21.7 us  [local(): sums = lax.all_to_all(sums, head_axes, 0, 0, tiled=True)]
    unnamed x26 -> x46, local copies, waits for them, and re-layouts: 6.67 us -> 16.1 us
    all_to_all x2, waiting for transfers between devices: 10.4 us -> 5.49 us  [scan(): return lax.all_to_all(sums, axes, 0, 0, tiled=True).reshape(state.shape)]
    pallas_call x8, Pallas kernels: 19.3 us -> 15 us  [call(): pl.pallas_call(kernel, out_shape=shapes, in_specs=specs, out_specs=out_sp...]
  transfers between devices with their start and end apart: 3 -> 3, of which waited for: 3 -> 2; matrix products, arithmetic and copies ran while one was open for 1% -> 1% of each run, Pallas kernels for 8% -> 8%
where the time goes in v2:
time: 106 us; the launch traced here: 104 us
  blocking collectives  36.6 us (35%)
  starting transfers between devices  19.8 us (19%)
  local copies, waits for them, and re-layouts  16.7 us (16%)
  Pallas kernels  15 us (14%)
  waiting for transfers between devices  14.7 us (14%)
  between operations  1.51 us (1%)
    all_to_all x1, blocking collectives, local(): sums = lax.all_to_all(sums, head_axes, 0, 0, tiled=True)  21.7 us
    unnamed x46, local copies, waits for them, and re-layouts  16.1 us
    pallas_call x8, Pallas kernels, call(): pl.pallas_call(kernel, out_shape=shapes, in_specs=specs, out_specs=out_sp...  15 us
    all_to_all x1, blocking collectives, scan(): mine = lax.all_to_all(pieces, axes, 0, 0, tiled=True)  14.9 us
    all_to_all x1, starting transfers between devices, scan(): mine = lax.all_to_all(pieces, axes, 0, 0, tiled=True)  10.6 us
    all_to_all x1, waiting for transfers between devices, scan(): mine = lax.all_to_all(pieces, axes, 0, 0, tiled=True)  9.24 us
    all_to_all x2, starting transfers between devices, scan(): return lax.all_to_all(sums, axes, 0, 0, tiled=True).reshape(state.shape)  9.11 us
    all_to_all x2, waiting for transfers between devices, scan(): return lax.all_to_all(sums, axes, 0, 0, tiled=True).reshape(state.shape)  5.49 us
  transfers between devices with their start and end apart: 3, of which 2 were waited for; matrix products, arithmetic and copies ran while one was open for 1% of the time, Pallas kernels for 8%

profile of v2, /device:TPU:1, one launch (start us, length us, event | category | flops | bytes accessed | tf_op | source)
XLA Modules:
  0.0 104.3 jit_solution(4086635875248911426)
XLA Ops:
  0.6 0.0 copy-start
  0.6 1.0 copy-done
  1.7 1.0 copy-done.2
  2.7 0.7 copy-done.19
  3.4 1.8 %state.1 = f32[512,128]{1,0:T(8,128)} custom-call(f32[4]{0:T(128)S(1)} %copy-done.19, bf16[512,512]{1,0:T(8,128)(2,1)S(1)} %copy-done, bf16[512,512]{1,0:T(8,128)(2,1)S(1)} %copy-done.2), custom_call_target="tpu_custom_call" | custom-call | flops 134217728 | bytes 1048576 | tf_op jit(solution)/shard_map/state/pallas_call | solution.py:217
  5.2 0.0 copy-start.17
  5.2 10.6 %all-to-all-start = ((f32[32,16,128]{2,1,0:T(8,128)}), f32[32,16,128]{2,1,0:T(8,128)S(1)}, u32[]{:S(2)}, u32[]{:S(2)}) async-start(f32[32,16,128]{2,1,0:T(8,128)} %bitcast.2), calls=%async_computation | async-start | bytes 524288 | tf_op jit(solution)/shard_map/all_to_all | solution.py:233
  15.8 0.0 copy-start.20
  15.9 0.6 copy-done.20
  16.5 0.6 dynamic_slice.3
  17.8 9.2 %all-to-all-done.in_ref = f32[32,16,128]{2,1,0:T(8,128)S(1)} async-done(((f32[32,16,128]{2,1,0:T(8,128)}), f32[32,16,128]{2,1,0:T(8,128)S(1)}, u32[]{:S(2)}, u32[]{:S(2)}) %all-to-all-start) | async-done | bytes 262176 | tf_op jit(solution)/shard_map/all_to_all | solution.py:233
  27.0 0.8 scan.2
  27.8 4.8 %all-to-all-start.1 = ((f32[32,16,128]{2,1,0:T(8,128)}), f32[32,16,128]{2,1,0:T(8,128)S(1)}, u32[]{:S(2)}, u32[]{:S(2)}) async-start(f32[32,16,128]{2,1,0:T(8,128)} %scan.2), calls=%async_computation.1 | async-start | bytes 524288 | tf_op jit(solution)/shard_map/all_to_all | solution.py:241
  32.6 0.0 copy-done.17
  32.6 0.0 copy-done.1
  32.6 0.0 copy-done.3
  32.6 0.0 copy-start.4
  32.6 2.9 %inner.1 = (f32[512,512]{1,0:T(8,128)S(1)}, f32[512,512]{1,0:T(8,128)S(1)}, bf16[1024,512]{1,0:T(8,128)(2,1)S(1)}) custom-call(f32[4]{0:T(128)S(1)} %copy-done.20, bf16[512,512]{1,0:T(8,128)(2,1)S(1)} %copy-done.17, bf16[512,512]{1,0:T(8,128)(2,1)S(1)} %copy-done.1, bf16[512,512]{1,0:T(8,128)(2,1)S(1)} %copy-done.3), custom_call_target="tpu_custom_call" | custom-call | flops 536870912 | bytes 4718592 | tf_op jit(solution)/shard_map/inner/pallas_call | solution.py:217
  35.5 0.0 copy-start.11
  35.5 1.0 copy-done.11
  36.5 1.0 copy-done.15
  37.5 5.5 %all-to-all-done.1 = f32[32,16,128]{2,1,0:T(8,128)S(1)} async-done(((f32[32,16,128]{2,1,0:T(8,128)}), f32[32,16,128]{2,1,0:T(8,128)S(1)}, u32[]{:S(2)}, u32[]{:S(2)}) %all-to-all-start.1) | async-done | bytes 262176 | tf_op jit(solution)/shard_map/all_to_all | solution.py:241
  43.0 0.0 copy-done.4
  43.0 0.7 copy-done.18
  43.7 1.2 %copy-done.12 = f32[512,512]{1,0:T(8,128)S(1)} copy-done((f32[512,512]{1,0:T(8,128)S(1)}, f32[512,512]{1,0:T(8,128)}, u32[]{:S(2)}) %copy-start.12) | copy-done | bytes 1048600
  44.9 0.6 attend.1
  45.4 0.0 copy-start.13
  45.4 21.7 %all_to_all.25.sums_ref = f32[16,8,128]{2,1,0:T(8,128)S(1)} all-to-all(f32[16,8,128]{2,1,0:T(8,128)S(1)} %get-tuple-element.22), channel_id=1, replica_groups=mesh['y'=8,'x'=4,'z'=8,'c'=2] {'z','c'}, dimensions={0} | all-to-all | bytes 131072 | tf_op jit(solution)/shard_map/all_to_all | solution.py:280
  67.1 0.0 copy-done.16
  67.1 0.9 norm.1
  68.0 0.0 copy-done.13
  68.0 0.0 copy-start.21
  68.0 14.9 %all_to_all.26.in_ref = f32[32,16,128]{2,1,0:T(8,128)S(1)} all-to-all(f32[32,16,128]{2,1,0:T(8,128)S(1)} %bitcast.9), channel_id=1, replica_groups=mesh['y'=8,'x'=4,'z'=8,'c'=2] {'y','x'}, dimensions={0} | all-to-all | bytes 524288 | tf_op jit(solution)/shard_map/all_to_all | solution.py:233
  83.0 0.0 copy-done.21
  83.0 0.8 scan.3
  83.7 4.3 %all-to-all-start.4 = ((f32[32,16,128]{2,1,0:T(8,128)}), f32[32,16,128]{2,1,0:T(8,128)S(1)}, u32[]{:S(2)}, u32[]{:S(2)}) async-start(f32[32,16,128]{2,1,0:T(8,128)} %scan.3), calls=%async_computation.4 | async-start | bytes 524288 | tf_op jit(solution)/shard_map/all_to_all | solution.py:241
  88.1 0.0 copy-start.14
  88.1 1.2 %copy-done.14 = f32[512,512]{1,0:T(8,128)S(1)} copy-done((f32[512,512]{1,0:T(8,128)S(1)}, f32[512,512]{1,0:T(8,128)}, u32[]{:S(2)}) %copy-start.14) | copy-done | bytes 1048600
  89.3 1.0 copy-done.22
  90.3 5.7 %back.1 = (bf16[512,512]{1,0:T(8,128)(2,1)}, bf16[512,512]{1,0:T(8,128)(2,1)}, f32[512,512]{1,0:T(8,128)S(1)}, f32[512,512]{1,0:T(8,128)S(1)}, f32[512,512]{1,0:T(8,128)S(1)}) custom-call(f32[4]{0:T(128)S(1)} %copy-done.20, bf16[512,512]{1,0:T(8,128)(2,1)S(1)} %copy-done.17, bf16[512,512]{1,0:T(8,128)(2,1)S(1)} %copy-done.1, bf16[512,512]{1,0:T(8,128)(2,1)S(1)} %copy-done.3, ...), custom_call_target="tpu_custom_call" | custom-call | flops 1342177280 | bytes 8388608 | tf_op jit(solution)/shard_map/back/pallas_call | solution.py:217
  96.1 1.0 copy-done.5
  97.1 1.0 copy-done.7
  98.0 1.0 copy-done.9
  99.0 0.0 all-to-all-done.4
  99.0 1.2 %copy-done.6 = f32[512,512]{1,0:T(8,128)S(1)} copy-done((f32[512,512]{1,0:T(8,128)S(1)}, f32[512,512]{1,0:T(8,128)}, u32[]{:S(2)}) %copy-start.6) | copy-done | bytes 1048600
  100.2 1.2 %copy-done.8 = f32[512,512]{1,0:T(8,128)S(1)} copy-done((f32[512,512]{1,0:T(8,128)S(1)}, f32[512,512]{1,0:T(8,128)}, u32[]{:S(2)}) %copy-start.8) | copy-done | bytes 1048600
  101.5 1.2 %copy-done.10 = f32[512,512]{1,0:T(8,128)S(1)} copy-done((f32[512,512]{1,0:T(8,128)S(1)}, f32[512,512]{1,0:T(8,128)}, u32[]{:S(2)}) %copy-start.10) | copy-done | bytes 1048600
  102.7 1.6 %final.1 = (bf16[512,512]{1,0:T(8,128)(2,1)}, bf16[512,512]{1,0:T(8,128)(2,1)}) custom-call(bf16[512,512]{1,0:T(8,128)(2,1)S(1)} %copy-done.1, bf16[512,512]{1,0:T(8,128)(2,1)S(1)} %copy-done.3, f32[512,128]{1,0:T(8,128)S(1)} %bitcast.8, f32[512,512]{1,0:T(8,128)S(1)} %copy-done.6, f32[512,512]{1,0:T(8,128)S(1)} %copy-done.8, f32[512,512]{1,0:T(8,128)S(1)} %copy-done.10), custom_call_target="tpu_custom_call" | custom-call | flops 268435456 | bytes 5242880 | tf_op jit(solution)/shard_map/final/pallas_call | solution.py:217
  (16 shorter events, 0.0 us)
Async XLA Ops:
  0.6 1.0 %copy-start = (bf16[512,512]{1,0:T(8,128)(2,1)S(1)}, bf16[512,512]{1,0:T(8,128)(2,1)}, u32[]{:S(2)}) copy-start(bf16[512,512]{1,0:T(8,128)(2,1)} %k_ref.5) | copy-start | bytes 1572868
  1.7 1.0 copy-start.2
  2.7 0.7 copy-start.19
  5.2 27.4 %copy-start.17 = (bf16[512,512]{1,0:T(8,128)(2,1)S(1)}, bf16[512,512]{1,0:T(8,128)(2,1)}, u32[]{:S(2)}) copy-start(bf16[512,512]{1,0:T(8,128)(2,1)} %q_ref.5) | copy-start | bytes 1572868
  5.2 21.8 %all-to-all-start = ((f32[32,16,128]{2,1,0:T(8,128)}), f32[32,16,128]{2,1,0:T(8,128)S(1)}, u32[]{:S(2)}, u32[]{:S(2)}) async-start(f32[32,16,128]{2,1,0:T(8,128)} %bitcast.2), calls=%async_computation | async-start | bytes 524288 | tf_op jit(solution)/shard_map/all_to_all | solution.py:233
  15.8 0.7 copy-start.20
  27.0 5.6 %copy-start.1 = (bf16[512,512]{1,0:T(8,128)(2,1)S(1)}, bf16[512,512]{1,0:T(8,128)(2,1)}, u32[]{:S(2)}) copy-start(bf16[512,512]{1,0:T(8,128)(2,1)} %k_ref.5) | copy-start | bytes 1572868
  27.0 5.6 %copy-start.3 = (bf16[512,512]{1,0:T(8,128)(2,1)S(1)}, bf16[512,512]{1,0:T(8,128)(2,1)}, u32[]{:S(2)}) copy-start(bf16[512,512]{1,0:T(8,128)(2,1)} %v_ref.5) | copy-start | bytes 1572868
  27.8 15.2 %all-to-all-start.1 = ((f32[32,16,128]{2,1,0:T(8,128)}), f32[32,16,128]{2,1,0:T(8,128)S(1)}, u32[]{:S(2)}, u32[]{:S(2)}) async-start(f32[32,16,128]{2,1,0:T(8,128)} %scan.2), calls=%async_computation.1 | async-start | bytes 524288 | tf_op jit(solution)/shard_map/all_to_all | solution.py:241
  32.6 10.4 %copy-start.4 = (bf16[512,512]{1,0:T(8,128)(2,1)S(1)}, bf16[512,512]{1,0:T(8,128)(2,1)}, u32[]{:S(2)}) copy-start(bf16[512,512]{1,0:T(8,128)(2,1)} %g_ref.3) | copy-start | bytes 1572868
  35.5 1.0 copy-start.11
  36.5 1.0 copy-start.15
  43.0 0.7 copy-start.18
  43.6 1.2 %copy-start.12 = (f32[512,512]{1,0:T(8,128)S(1)}, f32[512,512]{1,0:T(8,128)}, u32[]{:S(2)}) copy-start(f32[512,512]{1,0:T(8,128)} %copy-done.11) | copy-start | bytes 3145732
  44.9 22.3 %copy-start.16 = (bf16[1024,512]{1,0:T(8,128)(2,1)S(1)}, bf16[1024,512]{1,0:T(8,128)(2,1)}, u32[]{:S(2)}) copy-start(bf16[1024,512]{1,0:T(8,128)(2,1)} %copy-done.15) | copy-start | bytes 3145732
  45.4 22.6 %copy-start.13 = (f32[512,512]{1,0:T(8,128)}, f32[512,512]{1,0:T(8,128)S(1)}, u32[]{:S(2)}) copy-start(f32[512,512]{1,0:T(8,128)S(1)} %get-tuple-element.20.att_ref) | copy-start | bytes 3145732
  68.0 14.9 %copy-start.21 = (bf16[512,512]{1,0:T(8,128)(2,1)}, bf16[512,512]{1,0:T(8,128)(2,1)S(1)}, u32[]{:S(2)}) copy-start(bf16[512,512]{1,0:T(8,128)(2,1)S(1)} %get-tuple-element.23.d_ref) | copy-start | bytes 1572868
  83.7 15.3 %all-to-all-start.4 = ((f32[32,16,128]{2,1,0:T(8,128)}), f32[32,16,128]{2,1,0:T(8,128)S(1)}, u32[]{:S(2)}, u32[]{:S(2)}) async-start(f32[32,16,128]{2,1,0:T(8,128)} %scan.3), calls=%async_computation.4 | async-start | bytes 524288 | tf_op jit(solution)/shard_map/all_to_all | solution.py:241
  88.1 1.2 %copy-start.14 = (f32[512,512]{1,0:T(8,128)S(1)}, f32[512,512]{1,0:T(8,128)}, u32[]{:S(2)}) copy-start(f32[512,512]{1,0:T(8,128)} %copy-done.13) | copy-start | bytes 3145732
  89.3 1.0 copy-start.22
  96.1 1.0 copy-start.5
  97.1 1.0 copy-start.7
  98.0 1.0 copy-start.9
  99.0 1.2 %copy-start.6 = (f32[512,512]{1,0:T(8,128)S(1)}, f32[512,512]{1,0:T(8,128)}, u32[]{:S(2)}) copy-start(f32[512,512]{1,0:T(8,128)} %copy-done.5) | copy-start | bytes 3145732
  100.2 1.2 %copy-start.8 = (f32[512,512]{1,0:T(8,128)S(1)}, f32[512,512]{1,0:T(8,128)}, u32[]{:S(2)}) copy-start(f32[512,512]{1,0:T(8,128)} %copy-done.7) | copy-start | bytes 3145732
  101.5 1.2 %copy-start.10 = (f32[512,512]{1,0:T(8,128)S(1)}, f32[512,512]{1,0:T(8,128)}, u32[]{:S(2)}) copy-start(f32[512,512]{1,0:T(8,128)} %copy-done.9) | copy-start | bytes 3145732

commit v3 on v2

v3 whole, which is shorter than its diff:
```python
import functools

import jax
import jax.numpy as jnp
from jax import lax
from jax.experimental import pallas as pl
from jax.experimental.pallas import tpu as pltpu
from jax.sharding import Mesh, PartitionSpec as P

DH = 128
TILE = 128
F32 = jnp.float32
BF16 = jnp.bfloat16
NT = (((1,), (1,)), ((), ()))
TN = (((0,), (0,)), ((), ()))
NN = (((1,), (0,)), ((), ()))
VMEM = pl.BlockSpec(memory_space=pltpu.VMEM)
SMEM = pl.BlockSpec(memory_space=pltpu.SMEM)
ANY = pl.BlockSpec(memory_space=pl.ANY)


def dot(left, right, dims):
    return lax.dot_general(left, right, dims, preferred_element_type=F32)


def halves(value):
    high = value.astype(BF16)
    return high, (value - high.astype(F32)).astype(BF16)


def dot_wide(left, right):
    return dot(
        jnp.concatenate([left, left], axis=1), jnp.concatenate(halves(right), axis=0), NN
    )


def rising(rate, count):
    step = lax.broadcasted_iota(jnp.int32, (8, DH), 0).astype(F32)
    table, size = jnp.exp(-rate * step), 8
    while size < count:
        table = jnp.concatenate([table, table * jnp.exp(-rate * size)], axis=0)
        size *= 2
    return table


def falling(rate, count):
    step = 8.0 - lax.broadcasted_iota(jnp.int32, (8, DH), 0).astype(F32)
    table, size = jnp.exp(-rate * step), 8
    while size < count:
        table = jnp.concatenate([table * jnp.exp(-rate * size), table], axis=0)
        size *= 2
    return table


def band(rate, count):
    row = lax.broadcasted_iota(jnp.int32, (TILE, count), 0) + (count - TILE)
    diff = (row - lax.broadcasted_iota(jnp.int32, (TILE, count), 1)).astype(F32)
    wide = jnp.concatenate([rate] * (count // DH), axis=1)
    return jnp.where(diff >= 0, jnp.exp(-wide * jnp.maximum(diff, 0.0)), 0.0)


def fetch(pairs, sems):
    copies = [
        pltpu.make_async_copy(far, near, sems.at[i]) for i, (far, near) in enumerate(pairs)
    ]
    for copy in copies:
        copy.start()
    return copies


def wait(copies):
    for copy in copies:
        copy.wait()


def head(h):
    return slice(h * DH, (h + 1) * DH)


def diagonal():
    return lax.broadcasted_iota(jnp.int32, (TILE, TILE), 0) == lax.broadcasted_iota(
        jnp.int32, (TILE, TILE), 1
    )


def to_rows(part):
    sums = jnp.sum(part, axis=1, keepdims=True)
    mask = diagonal()
    return [
        jnp.sum(jnp.where(mask, sums[a * TILE : (a + 1) * TILE, :], 0.0), axis=0, keepdims=True)
        for a in range(part.shape[0] // TILE)
    ]


def to_columns(table, first, tiles):
    mask = diagonal()
    return jnp.concatenate(
        [
            jnp.sum(jnp.where(mask, table[a : a + 1, :], 0.0), axis=1, keepdims=True)
            for a in range(first, first + tiles)
        ],
        axis=0,
    )


def state_kernel(rate_hbm, k_hbm, v_hbm, out_ref, rate_ref, k_ref, v_ref, sems):
    count = k_ref.shape[0]
    copies = fetch(((rate_hbm, rate_ref), (k_hbm, k_ref), (v_hbm, v_ref)), sems)
    wait(copies)
    for h in range(rate_ref.shape[0]):
        rate = jnp.full((1, DH), rate_ref[h], F32)
        weight = falling(rate, count) * jnp.exp(rate)
        both = jnp.concatenate(halves(v_ref[:, head(h)].astype(F32) * weight), axis=1)
        sums = dot(k_ref[:, head(h)], both, TN)
        out_ref[head(h), :] = sums[:, :DH] + sums[:, DH:]


def scan_kernel(reverse, decay_ref, in_ref, out_ref):
    blocks = in_ref.shape[0]
    decay = decay_ref[...]
    total = jnp.zeros(in_ref.shape[1:], F32)
    order = range(blocks - 1, -1, -1) if reverse else range(blocks)
    for b in order:
        out_ref[b] = total
        total = total * decay + in_ref[b]


def inner_kernel(aux_ref, q_hbm, k_hbm, v_hbm, out_ref, q_ref, k_ref, v_ref, sems):
    count, width = k_ref.shape
    wait(fetch(((q_hbm, q_ref), (k_hbm, k_ref), (v_hbm, v_ref)), sems))
    for h in range(width // DH):
        table = band(aux_ref[1:2, head(h)], count)
        for a in range(count // TILE):
            here = slice(a * TILE, (a + 1) * TILE)
            seen = (a + 1) * TILE
            scores = dot(q_ref[here, head(h)], k_ref[:seen, head(h)], NT)
            weights = (scores * table[:, count - seen :]).astype(BF16)
            out_ref[here, head(h)] = dot(weights, v_ref[:seen, head(h)], NN)


def attend_kernel(aux_ref, q_ref, g_ref, inner_ref, prefix_ref, att_ref, sums_ref):
    count, width = q_ref.shape
    squares = jnp.zeros((count, DH), F32)
    crossing = jnp.zeros((count, DH), F32)
    for h in range(width // DH):
        rate = aux_ref[1:2, head(h)]
        weight = rising(rate, count) * jnp.exp(-rate)
        attended = (
            inner_ref[:, head(h)] + dot_wide(q_ref[:, head(h)], prefix_ref[head(h), :]) * weight
        )
        att_ref[:, head(h)] = attended
        squares += attended * attended
        crossing += g_ref[:, head(h)].astype(F32) * aux_ref[0:1, head(h)] * attended
    both = jnp.concatenate(to_rows(squares) + to_rows(crossing), axis=0)
    for j in range(sums_ref.shape[0]):
        sums_ref[j] = both


def turn_kernel(q_hbm, out_ref, q_ref, sems):
    wait(fetch(((q_hbm, q_ref),), sems))
    for h in range(q_ref.shape[1] // DH):
        out_ref[head(h), :] = q_ref[:, head(h)].T


def norm_scales(total, sums_ref):
    tiles = sums_ref.shape[1] // 2
    table = jnp.sum(sums_ref[...], axis=0) / total
    rinv = lax.rsqrt(table[:tiles, :] + 1e-06)
    factor = rinv * rinv * rinv * table[tiles:, :]
    return rinv, factor, tiles


def norm_kernel(
    total, aux_ref, turned_ref, g_ref, att_ref, sums_ref, grad_ref, state_ref
):
    count, width = g_ref.shape
    rinv, factor, tiles = norm_scales(total, sums_ref)
    rinv, factor = to_columns(rinv, 0, tiles), to_columns(factor, 0, tiles)
    for h in range(width // DH):
        scaled = g_ref[:, head(h)].astype(F32) * aux_ref[0:1, head(h)]
        grad = (rinv * scaled - att_ref[:, head(h)] * factor).astype(BF16)
        grad_ref[:, head(h)] = grad
        weight = rising(aux_ref[1:2, head(h)], count)
        both = jnp.concatenate(halves(grad.astype(F32) * weight), axis=1)
        sums = dot(turned_ref[head(h), :], both, NN)
        state_ref[head(h), :] = sums[:, :DH] + sums[:, DH:]


def query_kernel(
    total, aux_ref, k_hbm, v_hbm, d_ref, prefix_ref, att_ref, sums_ref,
    normed_ref, dq_ref, k_ref, v_ref, sems,
):
    count, width = k_ref.shape
    copies = fetch(((k_hbm, k_ref), (v_hbm, v_ref)), sems)
    rinv, _, tiles = norm_scales(total, sums_ref)
    rinv = to_columns(rinv, 0, tiles)
    for h in range(width // DH):
        normed_ref[:, head(h)] = (att_ref[:, head(h)] * rinv * aux_ref[0:1, head(h)]).astype(BF16)
    wait(copies)
    for h in range(width // DH):
        rate = aux_ref[1:2, head(h)]
        table = band(rate, count)
        weight = rising(rate, count) * jnp.exp(-rate)
        past = dot_wide(d_ref[:, head(h)], prefix_ref[head(h), :].T) * weight
        for a in range(count // TILE):
            here = slice(a * TILE, (a + 1) * TILE)
            seen = (a + 1) * TILE
            scores = dot(d_ref[here, head(h)], v_ref[:seen, head(h)], NT)
            grads = (scores * table[:, count - seen :]).astype(BF16)
            dq_ref[here, head(h)] = (
                dot(grads, k_ref[:seen, head(h)], NN) + past[here, :]
            ).astype(BF16)


def back_kernel(aux_ref, q_hbm, k_hbm, v_hbm, d_ref, dk_ref, dv_ref, q_ref, k_ref, v_ref, sems):
    count, width = q_ref.shape
    wait(fetch(((q_hbm, q_ref), (k_hbm, k_ref), (v_hbm, v_ref)), sems))
    for h in range(width // DH):
        table = band(aux_ref[1:2, head(h)], count)
        for a in range(count // TILE):
            here = slice(a * TILE, (a + 1) * TILE)
            seen = (a + 1) * TILE
            part = table[:, count - seen :]
            q, d = q_ref[here, head(h)], d_ref[here, head(h)]
            weights = (dot(q, k_ref[:seen, head(h)], NT) * part).astype(BF16)
            grads = (dot(d, v_ref[:seen, head(h)], NT) * part).astype(BF16)
            dk, dv = dot(grads, q, TN), dot(weights, d, TN)
            if a:
                before = slice(0, a * TILE)
                dk_ref[before, head(h)] += dk[before, :]
                dv_ref[before, head(h)] += dv[before, :]
            dk_ref[here, head(h)] = dk[here, :]
            dv_ref[here, head(h)] = dv[here, :]


def final_kernel(
    aux_ref, k_ref, v_ref, suffix_ref, dk_ref, dv_ref, kout_hbm, vout_hbm, kout_ref, vout_ref, sems
):
    count, width = k_ref.shape
    copies = []
    for h in range(width // DH):
        tail = falling(aux_ref[1:2, head(h)], count)
        suffix = suffix_ref[head(h), :]
        kout_ref[:, head(h)] = (
            dk_ref[:, head(h)] + dot_wide(v_ref[:, head(h)], suffix.T) * tail
        ).astype(BF16)
        vout_ref[:, head(h)] = (
            dv_ref[:, head(h)] + dot_wide(k_ref[:, head(h)], suffix) * tail
        ).astype(BF16)
        for index, (held, out) in enumerate(((kout_ref, kout_hbm), (vout_ref, vout_hbm))):
            copy = pltpu.make_async_copy(
                held.at[:, head(h)], out.at[:, head(h)], sems.at[2 * h + index]
            )
            copy.start()
            copies.append(copy)
    wait(copies)


def call(kernel, shapes, specs, *args, name, flops, size, mib=8, out_specs=None, scratch=()):
    return pl.pallas_call(
        kernel,
        out_shape=shapes,
        in_specs=specs,
        out_specs=out_specs or tuple(VMEM for _ in shapes),
        scratch_shapes=scratch,
        compiler_params=pltpu.CompilerParams(vmem_limit_bytes=mib * 2**20),
        cost_estimate=pl.CostEstimate(flops=flops, bytes_accessed=size, transcendentals=0),
        name=name,
    )(*args)


def scan(state, decay, reverse):
    axes = ("y", "x")
    blocks = lax.axis_size(axes)
    pieces = state.reshape(blocks, -1, DH)
    mine = lax.all_to_all(pieces, axes, 0, 0, tiled=True)
    (sums,) = call(
        functools.partial(scan_kernel, reverse),
        (jax.ShapeDtypeStruct(mine.shape, F32),),
        [VMEM, VMEM],
        decay, mine,
        name="scan", flops=2 * mine.size, size=2 * mine.size * 4, mib=2,
    )
    return lax.all_to_all(sums, axes, 0, 0, tiled=True).reshape(state.shape)


def local(queries, keys, values, out_grad, decay_rate, gain):
    count, width = queries.shape
    heads = decay_rate.shape[0]
    ctx, head_axes = ("y", "x"), ("z", "c")
    shape = jax.ShapeDtypeStruct
    whole, state_shape = (count, width), (width, DH)
    aux = jnp.stack([gain, jnp.repeat(decay_rate, DH)])
    owner = lax.axis_index(ctx) * heads // lax.axis_size(ctx)
    decay = jnp.exp(-lax.dynamic_slice(decay_rate, (owner,), (1,)) * count)
    decay = jnp.broadcast_to(decay[None, :], (1, DH))
    pair = 2 * count * count * DH * heads
    wide = 4 * count * DH * DH * heads
    unit = count * width
    far_rate, far_q, far_k, far_v = (
        pltpu.with_memory_space_constraint(array, pltpu.HBM)
        for array in (decay_rate, queries, keys, values)
    )
    block = pltpu.VMEM(whole, BF16)
    (state,) = call(
        state_kernel, (shape(state_shape, F32),), [ANY] * 3, far_rate, far_k, far_v,
        name="state", flops=wide, size=4 * unit,
        scratch=[pltpu.SMEM((heads,), F32), block, block, pltpu.SemaphoreType.DMA((3,))],
    )
    prefix = scan(state, decay, False)
    (inner,) = call(
        inner_kernel, (shape(whole, F32),), [VMEM] + [ANY] * 3, aux, far_q, far_k, far_v,
        name="inner", flops=2 * pair, size=10 * unit,
        scratch=[block, block, block, pltpu.SemaphoreType.DMA((3,))],
    )
    groups = lax.axis_size(head_axes)
    attended, sums = call(
        attend_kernel,
        (shape(whole, F32), shape((groups, 2 * count // TILE, TILE), F32)), [VMEM] * 5,
        aux, queries, out_grad, inner, prefix,
        name="attend", flops=wide, size=12 * unit,
    )
    sums = lax.all_to_all(sums, head_axes, 0, 0, tiled=True)
    (turned,) = call(
        turn_kernel, (shape((width, count), BF16),), [ANY], far_q,
        name="turn", flops=pair, size=4 * unit, mib=4,
        scratch=[block, pltpu.SemaphoreType.DMA((1,))],
    )
    total = float(heads * groups * DH)
    grad, state = call(
        functools.partial(norm_kernel, total),
        (shape(whole, BF16), shape(state_shape, F32)), [VMEM] * 5,
        aux, turned, out_grad, attended, sums,
        name="norm", flops=wide, size=12 * unit,
    )
    normed, dq = call(
        functools.partial(query_kernel, total),
        (shape(whole, BF16), shape(whole, BF16)), [VMEM] + [ANY] * 2 + [VMEM] * 4,
        aux, far_k, far_v, grad, prefix, attended, sums,
        name="query", flops=2 * pair, size=16 * unit,
        scratch=[block, block, pltpu.SemaphoreType.DMA((2,))],
    )
    decay, normed, dq = lax.optimization_barrier((decay, normed, dq))
    suffix = scan(state, decay, True)
    dk, dv = call(
        back_kernel, (shape(whole, F32), shape(whole, F32)), [VMEM] + [ANY] * 3 + [VMEM],
        aux, far_q, far_k, far_v, grad,
        name="back", flops=4 * pair, size=16 * unit,
        scratch=[block, block, block, pltpu.SemaphoreType.DMA((3,))],
    )
    dk, dv = call(
        final_kernel, (shape(whole, BF16), shape(whole, BF16)), [VMEM] * 6,
        aux, keys, values, suffix, dk, dv,
        name="final", flops=2 * wide, size=20 * unit, out_specs=(ANY, ANY),
        scratch=[block, block, pltpu.SemaphoreType.DMA((2 * heads,))],
    )
    return normed, dq, dk, dv


def solution(mesh):
    fine = Mesh(mesh.devices.reshape(8, 4, 8, 2), ("y", "x", "z", "c"))
    ctx, head_axes = ("y", "x"), ("z", "c")
    tokens = P(ctx, head_axes)
    return jax.shard_map(
        local,
        mesh=fine,
        in_specs=(tokens,) * 4 + (P(head_axes),) * 2,
        out_specs=(tokens,) * 4,
        check_vma=False,
    )
```

time: 106 us -> 100 us (0.943)
  the two profiles are of different devices: /device:TPU:1 before, /device:TPU:8 now
where the time goes in v3:
time: 100 us; the launch traced here: 99.6 us
  waiting for transfers between devices  37 us (37%)
  starting transfers between devices  34.7 us (35%)
  Pallas kernels  23.3 us (23%)
  local copies, waits for them, and re-layouts  2.97 us (3%)
  between operations  1.48 us (1%)
    pallas_call x10, Pallas kernels, call(): pl.pallas_call(kernel, out_shape=shapes, in_specs=specs, out_specs=out_sp...  23.3 us
    all_to_all x2, waiting for transfers between devices, scan(): mine = lax.all_to_all(pieces, axes, 0, 0, tiled=True)  18.8 us
    all_to_all x2, starting transfers between devices, scan(): mine = lax.all_to_all(pieces, axes, 0, 0, tiled=True)  15.1 us
    all_to_all x2, waiting for transfers between devices, scan(): return lax.all_to_all(sums, axes, 0, 0, tiled=True).reshape(state.shape)  11.6 us
    all_to_all x1, starting transfers between devices, local(): sums = lax.all_to_all(sums, head_axes, 0, 0, tiled=True)  10.4 us
    all_to_all x2, starting transfers between devices, scan(): return lax.all_to_all(sums, axes, 0, 0, tiled=True).reshape(state.shape)  9.26 us
    all_to_all x1, waiting for transfers between devices, local(): sums = lax.all_to_all(sums, head_axes, 0, 0, tiled=True)  6.62 us
    unnamed x16, local copies, waits for them, and re-layouts  2.31 us
  transfers between devices with their start and end apart: 5, of which 5 were waited for; matrix products, arithmetic and copies ran while one was open for 1% of the time, Pallas kernels for 15%

profile of v3, /device:TPU:8, one launch (start us, length us, event | category | flops | bytes accessed | tf_op | source)
XLA Modules:
  0.0 99.6 jit_solution(4155206945928629219)
XLA Ops:
  0.6 2.4 %state.1 = f32[512,128]{1,0:T(8,128)} custom-call(f32[4]{0:T(128)} %rate_hbm.1, bf16[512,512]{1,0:T(8,128)(2,1)} %k_ref.1, bf16[512,512]{1,0:T(8,128)(2,1)} %v_ref.1), custom_call_target="tpu_custom_call" | custom-call | flops 134217728 | bytes 1048576 | tf_op jit(solution)/shard_map/state/pallas_call | solution.py:260
  3.1 10.2 %all-to-all-start = ((f32[32,16,128]{2,1,0:T(8,128)}), f32[32,16,128]{2,1,0:T(8,128)S(1)}, u32[]{:S(2)}, u32[]{:S(2)}) async-start(f32[32,16,128]{2,1,0:T(8,128)} %bitcast.3), calls=%async_computation | async-start | bytes 524288 | tf_op jit(solution)/shard_map/all_to_all | solution.py:276
  13.3 0.0 copy-start.6
  13.3 0.6 copy-done.6
  13.9 0.6 dynamic_slice.3
  15.2 10.2 %all-to-all-done.in_ref = f32[32,16,128]{2,1,0:T(8,128)S(1)} async-done(((f32[32,16,128]{2,1,0:T(8,128)}), f32[32,16,128]{2,1,0:T(8,128)S(1)}, u32[]{:S(2)}, u32[]{:S(2)}) %all-to-all-start) | async-done | bytes 262176 | tf_op jit(solution)/shard_map/all_to_all | solution.py:276
  25.4 0.8 scan.2
  26.2 4.6 %all-to-all-start.1 = ((f32[32,16,128]{2,1,0:T(8,128)}), f32[32,16,128]{2,1,0:T(8,128)S(1)}, u32[]{:S(2)}, u32[]{:S(2)}) async-start(f32[32,16,128]{2,1,0:T(8,128)} %scan.2), calls=%async_computation.1 | async-start | bytes 524288 | tf_op jit(solution)/shard_map/all_to_all | solution.py:284
  30.8 0.0 copy-start.7
  30.8 0.1 broadcast_in_dim.13
  30.9 0.6 copy-done.7
  31.5 0.0 copy-start.2
  31.5 0.0 copy-start.3
  31.5 3.7 %inner.1.inner_ref = f32[512,512]{1,0:T(8,128)S(1)} custom-call(f32[2,512]{1,0:T(2,128)S(1)} %pad_maximum_fusion.aux_ref, bf16[512,512]{1,0:T(8,128)(2,1)} %q_hbm.5, bf16[512,512]{1,0:T(8,128)(2,1)} %k_ref.1, bf16[512,512]{1,0:T(8,128)(2,1)} %v_ref.1), custom_call_target="tpu_custom_call" | custom-call | flops 536870912 | bytes 2621440 | tf_op jit(solution)/shard_map/inner/pallas_call | solution.py:260
  35.3 6.8 %all-to-all-done.1 = f32[32,16,128]{2,1,0:T(8,128)S(1)} async-done(((f32[32,16,128]{2,1,0:T(8,128)}), f32[32,16,128]{2,1,0:T(8,128)S(1)}, u32[]{:S(2)}, u32[]{:S(2)}) %all-to-all-start.1) | async-done | bytes 262176 | tf_op jit(solution)/shard_map/all_to_all | solution.py:284
  42.1 0.0 copy-done.2
  42.1 0.0 copy-done.3
  42.1 1.3 %attend.1 = (f32[512,512]{1,0:T(8,128)S(1)}, f32[16,8,128]{2,1,0:T(8,128)}) custom-call(f32[2,512]{1,0:T(2,128)S(1)} %pad_maximum_fusion.aux_ref, bf16[512,512]{1,0:T(8,128)(2,1)S(1)} %copy-done.2, bf16[512,512]{1,0:T(8,128)(2,1)S(1)} %copy-done.3, f32[512,512]{1,0:T(8,128)S(1)} %inner.1.inner_ref, f32[512,128]{1,0:T(8,128)S(1)} %bitcast.7), custom_call_target="tpu_custom_call" | custom-call | flops 134217728 | bytes 3145728 | tf_op jit(solution)/shard_map/attend/pallas_call | solution.py:260
  43.4 10.4 %all-to-all-start.2 = ((f32[16,8,128]{2,1,0:T(8,128)}), f32[16,8,128]{2,1,0:T(8,128)S(1)}, u32[]{:S(2)}, u32[]{:S(2)}) async-start(f32[16,8,128]{2,1,0:T(8,128)} %get-tuple-element.18), calls=%async_computation.2 | async-start | bytes 131072 | tf_op jit(solution)/shard_map/all_to_all | solution.py:323
  53.8 1.2 %turn.1.turned_ref = bf16[512,512]{1,0:T(8,128)(2,1)S(1)} custom-call(bf16[512,512]{1,0:T(8,128)(2,1)} %q_hbm.5), custom_call_target="tpu_custom_call" | custom-call | flops 268435456 | bytes 1048576 | tf_op jit(solution)/shard_map/turn/pallas_call | solution.py:260
  55.0 6.6 %all-to-all-done.2.sums_ref = f32[16,8,128]{2,1,0:T(8,128)S(1)} async-done(((f32[16,8,128]{2,1,0:T(8,128)}), f32[16,8,128]{2,1,0:T(8,128)S(1)}, u32[]{:S(2)}, u32[]{:S(2)}) %all-to-all-start.2) | async-done | bytes 65568 | tf_op jit(solution)/shard_map/all_to_all | solution.py:323
  61.7 1.6 %norm.1 = (bf16[512,512]{1,0:T(8,128)(2,1)S(1)}, f32[512,128]{1,0:T(8,128)}) custom-call(f32[2,512]{1,0:T(2,128)S(1)} %pad_maximum_fusion.aux_ref, bf16[512,512]{1,0:T(8,128)(2,1)S(1)} %turn.1.turned_ref, bf16[512,512]{1,0:T(8,128)(2,1)S(1)} %copy-done.3, f32[512,512]{1,0:T(8,128)S(1)} %get-tuple-element.17.att_ref, f32[16,8,128]{2,1,0:T(8,128)S(1)} %all-to-all-done.2.sums_ref), custom_call_target="tpu_custom_call" | custom-call | flops 134217728 | bytes 3145728 | tf_op jit(solution)/shard_map/norm/pallas_call | solution.py:260
  63.3 0.0 copy-start.4
  63.3 4.9 %all-to-all-start.3 = ((f32[32,16,128]{2,1,0:T(8,128)}), f32[32,16,128]{2,1,0:T(8,128)S(1)}, u32[]{:S(2)}, u32[]{:S(2)}) async-start(f32[32,16,128]{2,1,0:T(8,128)} %bitcast.5), calls=%async_computation.3 | async-start | bytes 524288 | tf_op jit(solution)/shard_map/all_to_all | solution.py:276
  68.1 4.4 %query.1 = (bf16[512,512]{1,0:T(8,128)(2,1)}, bf16[512,512]{1,0:T(8,128)(2,1)}) custom-call(f32[2,512]{1,0:T(2,128)S(1)} %pad_maximum_fusion.aux_ref, bf16[512,512]{1,0:T(8,128)(2,1)} %k_ref.1, bf16[512,512]{1,0:T(8,128)(2,1)} %v_ref.1, bf16[512,512]{1,0:T(8,128)(2,1)S(1)} %get-tuple-element.19.d_ref, f32[512,128]{1,0:T(8,128)S(1)} %bitcast.8, ...), custom_call_target="tpu_custom_call" | custom-call | flops 536870912 | bytes 4194304 | tf_op jit(solution)/shard_map/query/pallas_call | solution.py:260
  72.5 0.0 copy-done.4
  72.6 8.6 %all-to-all-done.3.in_ref = f32[32,16,128]{2,1,0:T(8,128)S(1)} async-done(((f32[32,16,128]{2,1,0:T(8,128)}), f32[32,16,128]{2,1,0:T(8,128)S(1)}, u32[]{:S(2)}, u32[]{:S(2)}) %all-to-all-start.3) | async-done | bytes 262176 | tf_op jit(solution)/shard_map/all_to_all | solution.py:276
  81.1 0.8 scan.3
  81.9 4.6 %all-to-all-start.4 = ((f32[32,16,128]{2,1,0:T(8,128)}), f32[32,16,128]{2,1,0:T(8,128)S(1)}, u32[]{:S(2)}, u32[]{:S(2)}) async-start(f32[32,16,128]{2,1,0:T(8,128)} %scan.3), calls=%async_computation.4 | async-start | bytes 524288 | tf_op jit(solution)/shard_map/all_to_all | solution.py:284
  86.6 0.0 copy-start.5
  86.6 1.0 %copy-done.5 = bf16[512,512]{1,0:T(8,128)(2,1)S(1)} copy-done((bf16[512,512]{1,0:T(8,128)(2,1)S(1)}, bf16[512,512]{1,0:T(8,128)(2,1)}, u32[]{:S(2)}) %copy-start.5) | copy-done | bytes 524312
  87.6 0.0 copy-start
  87.6 0.0 copy-start.1
  87.6 5.6 %back.1 = (f32[512,512]{1,0:T(8,128)S(1)}, f32[512,512]{1,0:T(8,128)S(1)}) custom-call(f32[2,512]{1,0:T(2,128)S(1)} %pad_maximum_fusion.aux_ref, bf16[512,512]{1,0:T(8,128)(2,1)} %q_hbm.5, bf16[512,512]{1,0:T(8,128)(2,1)} %k_ref.1, bf16[512,512]{1,0:T(8,128)(2,1)} %v_ref.1, bf16[512,512]{1,0:T(8,128)(2,1)S(1)} %copy-done.5), custom_call_target="tpu_custom_call" | custom-call | flops 1073741824 | bytes 4194304 | tf_op jit(solution)/shard_map/back/pallas_call | solution.py:260
  93.2 4.8 %all-to-all-done.4 = f32[32,16,128]{2,1,0:T(8,128)S(1)} async-done(((f32[32,16,128]{2,1,0:T(8,128)}), f32[32,16,128]{2,1,0:T(8,128)S(1)}, u32[]{:S(2)}, u32[]{:S(2)}) %all-to-all-start.4) | async-done | bytes 262176 | tf_op jit(solution)/shard_map/all_to_all | solution.py:284
  98.0 0.0 copy-done
  98.0 0.0 copy-done.1
  98.0 1.6 %final.1 = (bf16[512,512]{1,0:T(8,128)(2,1)}, bf16[512,512]{1,0:T(8,128)(2,1)}) custom-call(f32[2,512]{1,0:T(2,128)S(1)} %pad_maximum_fusion.aux_ref, bf16[512,512]{1,0:T(8,128)(2,1)S(1)} %copy-done, bf16[512,512]{1,0:T(8,128)(2,1)S(1)} %copy-done.1, f32[512,128]{1,0:T(8,128)S(1)} %bitcast.9, f32[512,512]{1,0:T(8,128)S(1)} %get-tuple-element.26.dk_ref, ...), custom_call_target="tpu_custom_call" | custom-call | flops 268435456 | bytes 5242880 | tf_op jit(solution)/shard_map/final/pallas_call | solution.py:260
  (2 shorter events, 0.0 us)
Async XLA Ops:
  3.1 22.3 %all-to-all-start = ((f32[32,16,128]{2,1,0:T(8,128)}), f32[32,16,128]{2,1,0:T(8,128)S(1)}, u32[]{:S(2)}, u32[]{:S(2)}) async-start(f32[32,16,128]{2,1,0:T(8,128)} %bitcast.3), calls=%async_computation | async-start | bytes 524288 | tf_op jit(solution)/shard_map/all_to_all | solution.py:276
  13.3 0.7 copy-start.6
  26.2 15.9 %all-to-all-start.1 = ((f32[32,16,128]{2,1,0:T(8,128)}), f32[32,16,128]{2,1,0:T(8,128)S(1)}, u32[]{:S(2)}, u32[]{:S(2)}) async-start(f32[32,16,128]{2,1,0:T(8,128)} %scan.2), calls=%async_computation.1 | async-start | bytes 524288 | tf_op jit(solution)/shard_map/all_to_all | solution.py:284
  30.8 0.7 copy-start.7
  31.5 10.6 %copy-start.2 = (bf16[512,512]{1,0:T(8,128)(2,1)S(1)}, bf16[512,512]{1,0:T(8,128)(2,1)}, u32[]{:S(2)}) copy-start(bf16[512,512]{1,0:T(8,128)(2,1)} %q_hbm.5) | copy-start | bytes 1572868
  31.5 10.6 %copy-start.3 = (bf16[512,512]{1,0:T(8,128)(2,1)S(1)}, bf16[512,512]{1,0:T(8,128)(2,1)}, u32[]{:S(2)}) copy-start(bf16[512,512]{1,0:T(8,128)(2,1)} %g_ref.3) | copy-start | bytes 1572868
  43.4 18.3 %all-to-all-start.2 = ((f32[16,8,128]{2,1,0:T(8,128)}), f32[16,8,128]{2,1,0:T(8,128)S(1)}, u32[]{:S(2)}, u32[]{:S(2)}) async-start(f32[16,8,128]{2,1,0:T(8,128)} %get-tuple-element.18), calls=%async_computation.2 | async-start | bytes 131072 | tf_op jit(solution)/shard_map/all_to_all | solution.py:323
  63.3 9.3 %copy-start.4 = (bf16[512,512]{1,0:T(8,128)(2,1)}, bf16[512,512]{1,0:T(8,128)(2,1)S(1)}, u32[]{:S(2)}) copy-start(bf16[512,512]{1,0:T(8,128)(2,1)S(1)} %get-tuple-element.19.d_ref) | copy-start | bytes 1572868
  63.3 17.9 %all-to-all-start.3 = ((f32[32,16,128]{2,1,0:T(8,128)}), f32[32,16,128]{2,1,0:T(8,128)S(1)}, u32[]{:S(2)}, u32[]{:S(2)}) async-start(f32[32,16,128]{2,1,0:T(8,128)} %bitcast.5), calls=%async_computation.3 | async-start | bytes 524288 | tf_op jit(solution)/shard_map/all_to_all | solution.py:276
  81.9 16.1 %all-to-all-start.4 = ((f32[32,16,128]{2,1,0:T(8,128)}), f32[32,16,128]{2,1,0:T(8,128)S(1)}, u32[]{:S(2)}, u32[]{:S(2)}) async-start(f32[32,16,128]{2,1,0:T(8,128)} %scan.3), calls=%async_computation.4 | async-start | bytes 524288 | tf_op jit(solution)/shard_map/all_to_all | solution.py:284
  86.6 1.0 %copy-start.5 = (bf16[512,512]{1,0:T(8,128)(2,1)S(1)}, bf16[512,512]{1,0:T(8,128)(2,1)}, u32[]{:S(2)}) copy-start(bf16[512,512]{1,0:T(8,128)(2,1)} %copy-done.4) | copy-start | bytes 1572868
  87.6 10.4 %copy-start = (bf16[512,512]{1,0:T(8,128)(2,1)S(1)}, bf16[512,512]{1,0:T(8,128)(2,1)}, u32[]{:S(2)}) copy-start(bf16[512,512]{1,0:T(8,128)(2,1)} %k_ref.1) | copy-start | bytes 1572868
  87.6 10.4 %copy-start.1 = (bf16[512,512]{1,0:T(8,128)(2,1)S(1)}, bf16[512,512]{1,0:T(8,128)(2,1)}, u32[]{:S(2)}) copy-start(bf16[512,512]{1,0:T(8,128)(2,1)} %v_ref.1) | copy-start | bytes 1572868

commit v4 on v3

--- a/solution.py
+++ b/solution.py
@@ -34,8 +34,8 @@
     )
 
 
-def rising(rate, count):
-    step = lax.broadcasted_iota(jnp.int32, (8, DH), 0).astype(F32)
+def rising(rate, count, first):
+    step = lax.broadcasted_iota(jnp.int32, (8, DH), 0).astype(F32) + first
     table, size = jnp.exp(-rate * step), 8
     while size < count:
         table = jnp.concatenate([table, table * jnp.exp(-rate * size)], axis=0)
@@ -43,8 +43,8 @@
     return table
 
 
-def falling(rate, count):
-    step = 8.0 - lax.broadcasted_iota(jnp.int32, (8, DH), 0).astype(F32)
+def falling(rate, count, last):
+    step = 7.0 + last - lax.broadcasted_iota(jnp.int32, (8, DH), 0).astype(F32)
     table, size = jnp.exp(-rate * step), 8
     while size < count:
         table = jnp.concatenate([table * jnp.exp(-rate * size), table], axis=0)
@@ -104,14 +104,20 @@
 
 
 def state_kernel(rate_hbm, k_hbm, v_hbm, out_ref, rate_ref, k_ref, v_ref, sems):
-    count = k_ref.shape[0]
-    copies = fetch(((rate_hbm, rate_ref), (k_hbm, k_ref), (v_hbm, v_ref)), sems)
-    wait(copies)
-    for h in range(rate_ref.shape[0]):
-        rate = jnp.full((1, DH), rate_ref[h], F32)
-        weight = falling(rate, count) * jnp.exp(rate)
-        both = jnp.concatenate(halves(v_ref[:, head(h)].astype(F32) * weight), axis=1)
-        sums = dot(k_ref[:, head(h)], both, TN)
+    count, width = k_ref.shape
+    copies = fetch(((rate_hbm, rate_ref), (v_hbm, v_ref), (k_hbm, k_ref)), sems)
+    copies[0].wait()
+    weights = [
+        falling(jnp.full((1, DH), rate_ref[h], F32), count, 0.0) for h in range(width // DH)
+    ]
+    copies[1].wait()
+    parts = [
+        jnp.concatenate(halves(v_ref[:, head(h)].astype(F32) * weights[h]), axis=1)
+        for h in range(width // DH)
+    ]
+    copies[2].wait()
+    for h in range(width // DH):
+        sums = dot(k_ref[:, head(h)], parts[h], TN)
         out_ref[head(h), :] = sums[:, :DH] + sums[:, DH:]
 
 
@@ -125,11 +131,14 @@
         total = total * decay + in_ref[b]
 
 
-def inner_kernel(aux_ref, q_hbm, k_hbm, v_hbm, out_ref, q_ref, k_ref, v_ref, sems):
+def inner_kernel(
+    aux_ref, q_hbm, k_hbm, v_hbm, out_ref, turned_ref, q_ref, k_ref, v_ref, sems
+):
     count, width = k_ref.shape
     wait(fetch(((q_hbm, q_ref), (k_hbm, k_ref), (v_hbm, v_ref)), sems))
     for h in range(width // DH):
         table = band(aux_ref[1:2, head(h)], count)
+        turned_ref[head(h), :] = q_ref[:, head(h)].T
         for a in range(count // TILE):
             here = slice(a * TILE, (a + 1) * TILE)
             seen = (a + 1) * TILE
@@ -144,7 +153,7 @@
     crossing = jnp.zeros((count, DH), F32)
     for h in range(width // DH):
         rate = aux_ref[1:2, head(h)]
-        weight = rising(rate, count) * jnp.exp(-rate)
+        weight = rising(rate, count, 1.0)
         attended = (
             inner_ref[:, head(h)] + dot_wide(q_ref[:, head(h)], prefix_ref[head(h), :]) * weight
         )
@@ -156,12 +165,6 @@
         sums_ref[j] = both
 
 
-def turn_kernel(q_hbm, out_ref, q_ref, sems):
-    wait(fetch(((q_hbm, q_ref),), sems))
-    for h in range(q_ref.shape[1] // DH):
-        out_ref[head(h), :] = q_ref[:, head(h)].T
-
-
 def norm_scales(total, sums_ref):
     tiles = sums_ref.shape[1] // 2
     table = jnp.sum(sums_ref[...], axis=0) / total
@@ -180,7 +183,7 @@
         scaled = g_ref[:, head(h)].astype(F32) * aux_ref[0:1, head(h)]
         grad = (rinv * scaled - att_ref[:, head(h)] * factor).astype(BF16)
         grad_ref[:, head(h)] = grad
-        weight = rising(aux_ref[1:2, head(h)], count)
+        weight = rising(aux_ref[1:2, head(h)], count, 0.0)
         both = jnp.concatenate(halves(grad.astype(F32) * weight), axis=1)
         sums = dot(turned_ref[head(h), :], both, NN)
         state_ref[head(h), :] = sums[:, :DH] + sums[:, DH:]
@@ -200,7 +203,7 @@
     for h in range(width // DH):
         rate = aux_ref[1:2, head(h)]
         table = band(rate, count)
-        weight = rising(rate, count) * jnp.exp(-rate)
+        weight = rising(rate, count, 1.0)
         past = dot_wide(d_ref[:, head(h)], prefix_ref[head(h), :].T) * weight
         for a in range(count // TILE):
             here = slice(a * TILE, (a + 1) * TILE)
@@ -239,7 +242,7 @@
     count, width = k_ref.shape
     copies = []
     for h in range(width // DH):
-        tail = falling(aux_ref[1:2, head(h)], count)
+        tail = falling(aux_ref[1:2, head(h)], count, 1.0)
         suffix = suffix_ref[head(h), :]
         kout_ref[:, head(h)] = (
             dk_ref[:, head(h)] + dot_wide(v_ref[:, head(h)], suffix.T) * tail
@@ -307,12 +310,14 @@
         name="state", flops=wide, size=4 * unit,
         scratch=[pltpu.SMEM((heads,), F32), block, block, pltpu.SemaphoreType.DMA((3,))],
     )
-    prefix = scan(state, decay, False)
-    (inner,) = call(
-        inner_kernel, (shape(whole, F32),), [VMEM] + [ANY] * 3, aux, far_q, far_k, far_v,
+    inner, turned = call(
+        inner_kernel, (shape(whole, F32), shape((width, count), BF16)), [VMEM] + [ANY] * 3,
+        aux, far_q, far_k, far_v,
         name="inner", flops=2 * pair, size=10 * unit,
         scratch=[block, block, block, pltpu.SemaphoreType.DMA((3,))],
     )
+    decay, inner, turned = lax.optimization_barrier((decay, inner, turned))
+    prefix = scan(state, decay, False)
     groups = lax.axis_size(head_axes)
     attended, sums = call(
         attend_kernel,
@@ -321,11 +326,6 @@
         name="attend", flops=wide, size=12 * unit,
     )
     sums = lax.all_to_all(sums, head_axes, 0, 0, tiled=True)
-    (turned,) = call(
-        turn_kernel, (shape((width, count), BF16),), [ANY], far_q,
-        name="turn", flops=pair, size=4 * unit, mib=4,
-        scratch=[block, pltpu.SemaphoreType.DMA((1,))],
-    )
     total = float(heads * groups * DH)
     grad, state = call(
         functools.partial(norm_kernel, total),
@@ -340,7 +340,6 @@
         name="query", flops=2 * pair, size=16 * unit,
         scratch=[block, block, pltpu.SemaphoreType.DMA((2,))],
     )
-    decay, normed, dq = lax.optimization_barrier((decay, normed, dq))
     suffix = scan(state, decay, True)
     dk, dv = call(
         back_kernel, (shape(whole, F32), shape(whole, F32)), [VMEM] + [ANY] * 3 + [VMEM],

time: 100 us -> 97.4 us (0.974)
  the two profiles are of different devices: /device:TPU:8 before, /device:TPU:1 now
where the time goes in v4:
time: 97.4 us; the launch traced here: 96.1 us
  blocking collectives  52.1 us (53%)
  Pallas kernels  19.9 us (20%)
  starting transfers between devices  14.9 us (15%)
  waiting for transfers between devices  4.08 us (4%)
  local copies, waits for them, and re-layouts  3.76 us (4%)
  between operations  1.49 us (2%)
    all_to_all x1, blocking collectives, local(): sums = lax.all_to_all(sums, head_axes, 0, 0, tiled=True)  21.2 us
    pallas_call x9, Pallas kernels, call(): pl.pallas_call(kernel, out_shape=shapes, in_specs=specs, out_specs=out_sp...  19.9 us
    all_to_all x1, blocking collectives, scan(): return lax.all_to_all(sums, axes, 0, 0, tiled=True).reshape(state.shape)  15.6 us
    all_to_all x1, blocking collectives, scan(): mine = lax.all_to_all(pieces, axes, 0, 0, tiled=True)  15.2 us
    all_to_all x1, starting transfers between devices, scan(): mine = lax.all_to_all(pieces, axes, 0, 0, tiled=True)  10.5 us
    all_to_all x1, starting transfers between devices, scan(): return lax.all_to_all(sums, axes, 0, 0, tiled=True).reshape(state.shape)  4.35 us
    all_to_all x1, waiting for transfers between devices, scan(): mine = lax.all_to_all(pieces, axes, 0, 0, tiled=True)  4.08 us
    unnamed x20, local copies, waits for them, and re-layouts  3.1 us
  transfers between devices with their start and end apart: 2, of which 1 were waited for; matrix products, arithmetic and copies ran while one was open for 1% of the time, Pallas kernels for 14%

profile of v4, /device:TPU:1, one launch (start us, length us, event | category | flops | bytes accessed | tf_op | source)
XLA Modules:
  0.0 96.1 jit_solution(11466598071938806827)
XLA Ops:
  0.6 2.3 %state.1 = f32[512,128]{1,0:T(8,128)} custom-call(f32[4]{0:T(128)} %rate_hbm.1, bf16[512,512]{1,0:T(8,128)(2,1)} %k_ref.1, bf16[512,512]{1,0:T(8,128)(2,1)} %v_ref.1), custom_call_target="tpu_custom_call" | custom-call | flops 134217728 | bytes 1048576 | tf_op jit(solution)/shard_map/state/pallas_call | solution.py:263
  3.0 10.5 %all-to-all-start = ((f32[32,16,128]{2,1,0:T(8,128)}), f32[32,16,128]{2,1,0:T(8,128)S(1)}, u32[]{:S(2)}, u32[]{:S(2)}) async-start(f32[32,16,128]{2,1,0:T(8,128)} %bitcast.3), calls=%async_computation | async-start | bytes 524288 | tf_op jit(solution)/shard_map/all_to_all | solution.py:279
  13.5 0.0 copy-start.8
  13.5 0.6 copy-done.8
  14.2 0.6 dynamic_slice.3
  15.4 0.0 copy-start.9
  15.5 0.1 broadcast_in_dim.11
  15.5 0.6 copy-done.9
  16.1 3.7 %inner.1 = (f32[512,512]{1,0:T(8,128)S(1)}, bf16[512,512]{1,0:T(8,128)(2,1)S(1)}) custom-call(f32[2,512]{1,0:T(2,128)S(1)} %pad_maximum_fusion.aux_ref, bf16[512,512]{1,0:T(8,128)(2,1)} %q_hbm.3, bf16[512,512]{1,0:T(8,128)(2,1)} %k_ref.1, bf16[512,512]{1,0:T(8,128)(2,1)} %v_ref.1), custom_call_target="tpu_custom_call" | custom-call | flops 536870912 | bytes 2621440 | tf_op jit(solution)/shard_map/inner/pallas_call | solution.py:263
  19.8 0.0 copy-start.4
  19.8 0.8 copy-done.4
  20.6 0.0 copy-start.2
  20.6 0.0 copy-start.3
  20.6 4.1 %all-to-all-done.in_ref = f32[32,16,128]{2,1,0:T(8,128)S(1)} async-done(((f32[32,16,128]{2,1,0:T(8,128)}), f32[32,16,128]{2,1,0:T(8,128)S(1)}, u32[]{:S(2)}, u32[]{:S(2)}) %all-to-all-start) | async-done | bytes 262176 | tf_op jit(solution)/shard_map/all_to_all | solution.py:279
  24.7 0.1 scan.2
  24.8 15.6 %all_to_all.25 = f32[32,16,128]{2,1,0:T(8,128)S(1)} all-to-all(f32[32,16,128]{2,1,0:T(8,128)S(1)} %scan.2), channel_id=1, replica_groups=mesh['y'=8,'x'=4,'z'=8,'c'=2] {'y','x'}, dimensions={0} | all-to-all | bytes 524288 | tf_op jit(solution)/shard_map/all_to_all | solution.py:287
  40.4 0.0 copy-done.2
  40.4 0.0 copy-done.3
  40.4 0.0 copy-start.5
  40.4 0.6 attend.1
  41.0 21.2 %all_to_all.26.sums_ref = f32[16,8,128]{2,1,0:T(8,128)S(1)} all-to-all(f32[16,8,128]{2,1,0:T(8,128)S(1)} %get-tuple-element.25), channel_id=1, replica_groups=mesh['y'=8,'x'=4,'z'=8,'c'=2] {'z','c'}, dimensions={0} | all-to-all | bytes 131072 | tf_op jit(solution)/shard_map/all_to_all | solution.py:328
  62.2 0.0 copy-done.5
  62.2 0.9 norm.1
  63.1 0.0 copy-start.6
  63.1 15.2 %all_to_all.27.in_ref = f32[32,16,128]{2,1,0:T(8,128)S(1)} all-to-all(f32[32,16,128]{2,1,0:T(8,128)S(1)} %bitcast.10), channel_id=1, replica_groups=mesh['y'=8,'x'=4,'z'=8,'c'=2] {'y','x'}, dimensions={0} | all-to-all | bytes 524288 | tf_op jit(solution)/shard_map/all_to_all | solution.py:279
  78.4 0.8 scan.3
  79.1 4.4 %all-to-all-start.4 = ((f32[32,16,128]{2,1,0:T(8,128)}), f32[32,16,128]{2,1,0:T(8,128)S(1)}, u32[]{:S(2)}, u32[]{:S(2)}) async-start(f32[32,16,128]{2,1,0:T(8,128)} %scan.3), calls=%async_computation.4 | async-start | bytes 524288 | tf_op jit(solution)/shard_map/all_to_all | solution.py:287
  83.5 0.0 copy-done.6
  83.5 4.4 %query.1 = (bf16[512,512]{1,0:T(8,128)(2,1)}, bf16[512,512]{1,0:T(8,128)(2,1)}) custom-call(f32[2,512]{1,0:T(2,128)S(1)} %pad_maximum_fusion.aux_ref, bf16[512,512]{1,0:T(8,128)(2,1)} %k_ref.1, bf16[512,512]{1,0:T(8,128)(2,1)} %v_ref.1, bf16[512,512]{1,0:T(8,128)(2,1)S(1)} %get-tuple-element.26.d_ref, f32[512,128]{1,0:T(8,128)S(1)} %bitcast.8, ...), custom_call_target="tpu_custom_call" | custom-call | flops 536870912 | bytes 4194304 | tf_op jit(solution)/shard_map/query/pallas_call | solution.py:263
  87.9 0.0 copy-start.7
  87.9 1.0 %copy-done.7 = bf16[512,512]{1,0:T(8,128)(2,1)S(1)} copy-done((bf16[512,512]{1,0:T(8,128)(2,1)S(1)}, bf16[512,512]{1,0:T(8,128)(2,1)}, u32[]{:S(2)}) %copy-start.7) | copy-done | bytes 524312
  89.0 0.0 copy-start
  89.0 0.0 copy-start.1
  89.0 5.6 %back.1 = (f32[512,512]{1,0:T(8,128)S(1)}, f32[512,512]{1,0:T(8,128)S(1)}) custom-call(f32[2,512]{1,0:T(2,128)S(1)} %pad_maximum_fusion.aux_ref, bf16[512,512]{1,0:T(8,128)(2,1)} %q_hbm.3, bf16[512,512]{1,0:T(8,128)(2,1)} %k_ref.1, bf16[512,512]{1,0:T(8,128)(2,1)} %v_ref.1, bf16[512,512]{1,0:T(8,128)(2,1)S(1)} %copy-done.7), custom_call_target="tpu_custom_call" | custom-call | flops 1073741824 | bytes 4194304 | tf_op jit(solution)/shard_map/back/pallas_call | solution.py:263
  94.5 0.0 all-to-all-done.4
  94.5 0.0 copy-done
  94.6 0.0 copy-done.1
  94.6 1.6 %final.1 = (bf16[512,512]{1,0:T(8,128)(2,1)}, bf16[512,512]{1,0:T(8,128)(2,1)}) custom-call(f32[2,512]{1,0:T(2,128)S(1)} %pad_maximum_fusion.aux_ref, bf16[512,512]{1,0:T(8,128)(2,1)S(1)} %copy-done, bf16[512,512]{1,0:T(8,128)(2,1)S(1)} %copy-done.1, f32[512,128]{1,0:T(8,128)S(1)} %bitcast.9, f32[512,512]{1,0:T(8,128)S(1)} %get-tuple-element.30.dk_ref, ...), custom_call_target="tpu_custom_call" | custom-call | flops 268435456 | bytes 5242880 | tf_op jit(solution)/shard_map/final/pallas_call | solution.py:263
  (2 shorter events, 0.0 us)
Async XLA Ops:
  3.0 21.7 %all-to-all-start = ((f32[32,16,128]{2,1,0:T(8,128)}), f32[32,16,128]{2,1,0:T(8,128)S(1)}, u32[]{:S(2)}, u32[]{:S(2)}) async-start(f32[32,16,128]{2,1,0:T(8,128)} %bitcast.3), calls=%async_computation | async-start | bytes 524288 | tf_op jit(solution)/shard_map/all_to_all | solution.py:279
  13.5 0.7 copy-start.8
  15.4 0.7 copy-start.9
  19.8 0.8 copy-start.4
  20.6 19.8 %copy-start.2 = (bf16[512,512]{1,0:T(8,128)(2,1)S(1)}, bf16[512,512]{1,0:T(8,128)(2,1)}, u32[]{:S(2)}) copy-start(bf16[512,512]{1,0:T(8,128)(2,1)} %g_ref.3) | copy-start | bytes 1572868
  20.6 19.8 %copy-start.3 = (bf16[512,512]{1,0:T(8,128)(2,1)S(1)}, bf16[512,512]{1,0:T(8,128)(2,1)}, u32[]{:S(2)}) copy-start(bf16[512,512]{1,0:T(8,128)(2,1)} %q_hbm.3) | copy-start | bytes 1572868
  40.4 21.8 %copy-start.5 = (bf16[512,512]{1,0:T(8,128)(2,1)S(1)}, bf16[512,512]{1,0:T(8,128)(2,1)}, u32[]{:S(2)}) copy-start(bf16[512,512]{1,0:T(8,128)(2,1)} %copy-done.4) | copy-start | bytes 1572868
  63.1 20.4 %copy-start.6 = (bf16[512,512]{1,0:T(8,128)(2,1)}, bf16[512,512]{1,0:T(8,128)(2,1)S(1)}, u32[]{:S(2)}) copy-start(bf16[512,512]{1,0:T(8,128)(2,1)S(1)} %get-tuple-element.26.d_ref) | copy-start | bytes 1572868
  79.1 15.4 %all-to-all-start.4 = ((f32[32,16,128]{2,1,0:T(8,128)}), f32[32,16,128]{2,1,0:T(8,128)S(1)}, u32[]{:S(2)}, u32[]{:S(2)}) async-start(f32[32,16,128]{2,1,0:T(8,128)} %scan.3), calls=%async_computation.4 | async-start | bytes 524288 | tf_op jit(solution)/shard_map/all_to_all | solution.py:287
  87.9 1.0 %copy-start.7 = (bf16[512,512]{1,0:T(8,128)(2,1)S(1)}, bf16[512,512]{1,0:T(8,128)(2,1)}, u32[]{:S(2)}) copy-start(bf16[512,512]{1,0:T(8,128)(2,1)} %copy-done.6) | copy-start | bytes 1572868
  89.0 5.6 %copy-start = (bf16[512,512]{1,0:T(8,128)(2,1)S(1)}, bf16[512,512]{1,0:T(8,128)(2,1)}, u32[]{:S(2)}) copy-start(bf16[512,512]{1,0:T(8,128)(2,1)} %k_ref.1) | copy-start | bytes 1572868
  89.0 5.6 %copy-start.1 = (bf16[512,512]{1,0:T(8,128)(2,1)S(1)}, bf16[512,512]{1,0:T(8,128)(2,1)}, u32[]{:S(2)}) copy-start(bf16[512,512]{1,0:T(8,128)(2,1)} %v_ref.1) | copy-start | bytes 1572868

commit v5 on v4

--- a/solution.py
+++ b/solution.py
@@ -5,10 +5,12 @@
 from jax import lax
 from jax.experimental import pallas as pl
 from jax.experimental.pallas import tpu as pltpu
-from jax.sharding import Mesh, PartitionSpec as P
+from jax.sharding import PartitionSpec as P
 
 DH = 128
 TILE = 128
+FIRST_CTX = 18
+FIRST_HEAD = 11
 F32 = jnp.float32
 BF16 = jnp.bfloat16
 NT = (((1,), (1,)), ((), ()))
@@ -103,13 +105,17 @@
     )
 
 
-def state_kernel(rate_hbm, k_hbm, v_hbm, out_ref, rate_ref, k_ref, v_ref, sems):
+def state_kernel(rate_hbm, k_hbm, v_hbm, out_ref, rows_ref, rate_ref, k_ref, v_ref, sems):
     count, width = k_ref.shape
     copies = fetch(((rate_hbm, rate_ref), (v_hbm, v_ref), (k_hbm, k_ref)), sems)
     copies[0].wait()
     weights = [
         falling(jnp.full((1, DH), rate_ref[h], F32), count, 0.0) for h in range(width // DH)
     ]
+    for h in range(width // DH):
+        rate = jnp.full((1, DH), rate_ref[h], F32)
+        rows_ref[1:2, head(h)] = rate
+        rows_ref[2:3, head(h)] = jnp.exp(-rate * count)
     copies[1].wait()
     parts = [
         jnp.concatenate(halves(v_ref[:, head(h)].astype(F32) * weights[h]), axis=1)
@@ -121,24 +127,28 @@
         out_ref[head(h), :] = sums[:, :DH] + sums[:, DH:]
 
 
-def scan_kernel(reverse, decay_ref, in_ref, out_ref):
+def scan_kernel(reverse, first, heads, aux_ref, in_ref, out_ref):
     blocks = in_ref.shape[0]
-    decay = decay_ref[...]
+    place = lax.rem(lax.axis_index("ctx") + (blocks - first), blocks)
+    owner = lax.div(place * heads, blocks)
+    decay = aux_ref[2:3, pl.ds(pl.multiple_of(owner * DH, DH), DH)]
     total = jnp.zeros(in_ref.shape[1:], F32)
     order = range(blocks - 1, -1, -1) if reverse else range(blocks)
     for b in order:
-        out_ref[b] = total
-        total = total * decay + in_ref[b]
+        place = (b - first) % blocks
+        out_ref[place] = total
+        total = total * decay + in_ref[place]
 
 
 def inner_kernel(
-    aux_ref, q_hbm, k_hbm, v_hbm, out_ref, turned_ref, q_ref, k_ref, v_ref, sems
+    rows_ref, gain_ref, q_hbm, k_hbm, v_hbm, out_ref, aux_ref, q_ref, k_ref, v_ref, sems
 ):
     count, width = k_ref.shape
+    aux_ref[...] = rows_ref[...]
+    aux_ref[0:1, :] = gain_ref[...]
     wait(fetch(((q_hbm, q_ref), (k_hbm, k_ref), (v_hbm, v_ref)), sems))
     for h in range(width // DH):
-        table = band(aux_ref[1:2, head(h)], count)
-        turned_ref[head(h), :] = q_ref[:, head(h)].T
+        table = band(rows_ref[1:2, head(h)], count)
         for a in range(count // TILE):
             here = slice(a * TILE, (a + 1) * TILE)
             seen = (a + 1) * TILE
@@ -174,7 +184,7 @@
 
 
 def norm_kernel(
-    total, aux_ref, turned_ref, g_ref, att_ref, sums_ref, grad_ref, state_ref
+    total, aux_ref, q_ref, g_ref, att_ref, sums_ref, grad_ref, state_ref
 ):
     count, width = g_ref.shape
     rinv, factor, tiles = norm_scales(total, sums_ref)
@@ -185,7 +195,7 @@
         grad_ref[:, head(h)] = grad
         weight = rising(aux_ref[1:2, head(h)], count, 0.0)
         both = jnp.concatenate(halves(grad.astype(F32) * weight), axis=1)
-        sums = dot(turned_ref[head(h), :], both, NN)
+        sums = dot(q_ref[:, head(h)], both, TN)
         state_ref[head(h), :] = sums[:, :DH] + sums[:, DH:]
 
 
@@ -272,31 +282,32 @@
     )(*args)
 
 
-def scan(state, decay, reverse):
-    axes = ("y", "x")
-    blocks = lax.axis_size(axes)
-    pieces = state.reshape(blocks, -1, DH)
-    mine = lax.all_to_all(pieces, axes, 0, 0, tiled=True)
+def exchange(pieces, axis, first):
+    size = lax.axis_size(axis)
+    order = [(first + j) % size for j in range(size)]
+    return lax.all_to_all(pieces, axis, 0, 0, tiled=True, axis_index_groups=[order])
+
+
+def scan(state, aux, heads, first, reverse):
+    pieces = state.reshape(lax.axis_size("ctx"), -1, DH)
+    mine = exchange(pieces, "ctx", first)
     (sums,) = call(
-        functools.partial(scan_kernel, reverse),
+        functools.partial(scan_kernel, reverse, first, heads),
         (jax.ShapeDtypeStruct(mine.shape, F32),),
         [VMEM, VMEM],
-        decay, mine,
+        aux, mine,
         name="scan", flops=2 * mine.size, size=2 * mine.size * 4, mib=2,
     )
-    return lax.all_to_all(sums, axes, 0, 0, tiled=True).reshape(state.shape)
+    return exchange(sums, "ctx", first).reshape(state.shape)
 
 
 def local(queries, keys, values, out_grad, decay_rate, gain):
     count, width = queries.shape
     heads = decay_rate.shape[0]
-    ctx, head_axes = ("y", "x"), ("z", "c")
     shape = jax.ShapeDtypeStruct
     whole, state_shape = (count, width), (width, DH)
-    aux = jnp.stack([gain, jnp.repeat(decay_rate, DH)])
-    owner = lax.axis_index(ctx) * heads // lax.axis_size(ctx)
-    decay = jnp.exp(-lax.dynamic_slice(decay_rate, (owner,), (1,)) * count)
-    decay = jnp.broadcast_to(decay[None, :], (1, DH))
+    groups = lax.axis_size("head")
+    middle, late = FIRST_CTX, FIRST_HEAD
     pair = 2 * count * count * DH * heads
     wide = 4 * count * DH * DH * heads
     unit = count * width
@@ -305,32 +316,30 @@
         for array in (decay_rate, queries, keys, values)
     )
     block = pltpu.VMEM(whole, BF16)
-    (state,) = call(
-        state_kernel, (shape(state_shape, F32),), [ANY] * 3, far_rate, far_k, far_v,
+    state, rows = call(
+        state_kernel, (shape(state_shape, F32), shape((8, width), F32)), [ANY] * 3, far_rate, far_k, far_v,
         name="state", flops=wide, size=4 * unit,
         scratch=[pltpu.SMEM((heads,), F32), block, block, pltpu.SemaphoreType.DMA((3,))],
     )
-    inner, turned = call(
-        inner_kernel, (shape(whole, F32), shape((width, count), BF16)), [VMEM] + [ANY] * 3,
-        aux, far_q, far_k, far_v,
+    inner, aux = call(
+        inner_kernel, (shape(whole, F32), shape((8, width), F32)), [VMEM] * 2 + [ANY] * 3,
+        rows, gain[None, :], far_q, far_k, far_v,
         name="inner", flops=2 * pair, size=10 * unit,
         scratch=[block, block, block, pltpu.SemaphoreType.DMA((3,))],
     )
-    decay, inner, turned = lax.optimization_barrier((decay, inner, turned))
-    prefix = scan(state, decay, False)
-    groups = lax.axis_size(head_axes)
+    prefix = scan(state, aux, heads, middle, False)
     attended, sums = call(
         attend_kernel,
         (shape(whole, F32), shape((groups, 2 * count // TILE, TILE), F32)), [VMEM] * 5,
         aux, queries, out_grad, inner, prefix,
         name="attend", flops=wide, size=12 * unit,
     )
-    sums = lax.all_to_all(sums, head_axes, 0, 0, tiled=True)
+    sums = exchange(sums, "head", late)
     total = float(heads * groups * DH)
     grad, state = call(
         functools.partial(norm_kernel, total),
         (shape(whole, BF16), shape(state_shape, F32)), [VMEM] * 5,
-        aux, turned, out_grad, attended, sums,
+        aux, queries, out_grad, attended, sums,
         name="norm", flops=wide, size=12 * unit,
     )
     normed, dq = call(
@@ -340,7 +349,8 @@
         name="query", flops=2 * pair, size=16 * unit,
         scratch=[block, block, pltpu.SemaphoreType.DMA((2,))],
     )
-    suffix = scan(state, decay, True)
+    aux, normed, dq = lax.optimization_barrier((aux, normed, dq))
+    suffix = scan(state, aux, heads, middle, True)
     dk, dv = call(
         back_kernel, (shape(whole, F32), shape(whole, F32)), [VMEM] + [ANY] * 3 + [VMEM],
         aux, far_q, far_k, far_v, grad,
@@ -357,13 +367,11 @@
 
 
 def solution(mesh):
-    fine = Mesh(mesh.devices.reshape(8, 4, 8, 2), ("y", "x", "z", "c"))
-    ctx, head_axes = ("y", "x"), ("z", "c")
-    tokens = P(ctx, head_axes)
+    tokens = P("ctx", "head")
     return jax.shard_map(
         local,
-        mesh=fine,
-        in_specs=(tokens,) * 4 + (P(head_axes),) * 2,
+        mesh=mesh,
+        in_specs=(tokens,) * 4 + (P("head"),) * 2,
         out_specs=(tokens,) * 4,
         check_vma=False,
     )

time: 97.4 us -> 92.8 us (0.953)
  blocking collectives: 52.1 us -> 34.6 us
  starting transfers between devices: 14.9 us -> 32.2 us
  local copies, waits for them, and re-layouts: 3.76 us -> 1.74 us
  waiting for transfers between devices: 4.08 us -> 2.27 us
    all_to_all x3 -> x2, blocking collectives: 52.1 us -> 34.6 us  [exchange(): lax.all_to_all(pieces, axis, 0, 0, tiled=True, axis_index_groups=[order])]
    all_to_all x2 -> x3, starting transfers between devices: 14.9 us -> 32.2 us  [exchange(): lax.all_to_all(pieces, axis, 0, 0, tiled=True, axis_index_groups=[order])]
    all_to_all x2 -> x3, waiting for transfers between devices: 4.08 us -> 2.27 us  [exchange(): lax.all_to_all(pieces, axis, 0, 0, tiled=True, axis_index_groups=[order])]
    unnamed x20 -> x14, local copies, waits for them, and re-layouts: 3.1 us -> 1.74 us
  transfers between devices with their start and end apart: 2 -> 3, of which waited for: 1 -> 1; matrix products, arithmetic and copies ran while one was open for 1% -> 0% of each run, Pallas kernels for 14% -> 15%
where the time goes in v5:
time: 92.8 us; the launch traced here: 92.2 us
  blocking collectives  34.6 us (37%)
  starting transfers between devices  32.2 us (35%)
  Pallas kernels  20.6 us (22%)
  waiting for transfers between devices  2.27 us (2%)
  local copies, waits for them, and re-layouts  1.74 us (2%)
    all_to_all x2, blocking collectives, exchange(): lax.all_to_all(pieces, axis, 0, 0, tiled=True, axis_index_groups=[order])  34.6 us
    all_to_all x3, starting transfers between devices, exchange(): lax.all_to_all(pieces, axis, 0, 0, tiled=True, axis_index_groups=[order])  32.2 us
    pallas_call x9, Pallas kernels, call(): pl.pallas_call(kernel, out_shape=shapes, in_specs=specs, out_specs=out_sp...  20.6 us
    all_to_all x3, waiting for transfers between devices, exchange(): lax.all_to_all(pieces, axis, 0, 0, tiled=True, axis_index_groups=[order])  2.27 us
  transfers between devices with their start and end apart: 3, of which 1 were waited for; matrix products, arithmetic and copies ran while one was open for 0% of the time, Pallas kernels for 15%

profile of v5, /device:TPU:1, one launch (start us, length us, event | category | flops | bytes accessed | tf_op | source)
XLA Modules:
  0.0 92.2 jit_solution(7414212286647187608)
XLA Ops:
  0.6 2.3 %state.1 = (f32[512,128]{1,0:T(8,128)}, f32[8,512]{1,0:T(8,128)S(1)}) custom-call(f32[4]{0:T(128)} %rate_hbm.1, bf16[512,512]{1,0:T(8,128)(2,1)} %k_ref.1, bf16[512,512]{1,0:T(8,128)(2,1)} %v_ref.1), custom_call_target="tpu_custom_call" | custom-call | flops 134217728 | bytes 1048576 | tf_op jit(solution)/shard_map/state/pallas_call | solution.py:273
  3.0 12.5 %all-to-all-start = ((f32[32,16,128]{2,1,0:T(8,128)}), f32[32,16,128]{2,1,0:T(8,128)S(1)}, u32[]{:S(2)}, u32[]{:S(2)}) async-start(f32[32,16,128]{2,1,0:T(8,128)} %bitcast.1), calls=%async_computation | async-start | bytes 524288 | tf_op jit(solution)/shard_map/all_to_all | solution.py:288
  15.4 0.0 copy-start.6
  15.4 0.7 copy-done.6
  16.1 3.7 %inner.1 = (f32[512,512]{1,0:T(8,128)S(1)}, f32[8,512]{1,0:T(8,128)S(1)}) custom-call(f32[8,512]{1,0:T(8,128)S(1)} %get-tuple-element.21.rows_ref, f32[1,512]{1,0:T(1,128)S(1)} %bitcast.8, bf16[512,512]{1,0:T(8,128)(2,1)} %q_hbm.3, bf16[512,512]{1,0:T(8,128)(2,1)} %k_ref.1, bf16[512,512]{1,0:T(8,128)(2,1)} %v_ref.1), custom_call_target="tpu_custom_call" | custom-call | flops 536870912 | bytes 2621440 | tf_op jit(solution)/shard_map/inner/pallas_call | solution.py:273
  19.8 0.0 all-to-all-done.in_ref
  19.8 0.0 copy-start.2
  19.8 0.0 copy-start.3
  19.8 0.1 scan.2
  19.9 13.4 %all_to_all.25 = f32[32,16,128]{2,1,0:T(8,128)S(1)} all-to-all(f32[32,16,128]{2,1,0:T(8,128)S(1)} %scan.2), channel_id=1, replica_groups={{288,304,320,336,352,368,384,400,416,432,448,464,480,496,0,16,32,48,64,..., dimensions={0} | all-to-all | bytes 524288 | tf_op jit(solution)/shard_map/all_to_all | solution.py:288
  33.3 0.0 copy-done.2
  33.3 0.0 copy-done.3
  33.3 0.6 attend.1
  33.9 21.2 %all_to_all.26.sums_ref = f32[16,8,128]{2,1,0:T(8,128)S(1)} all-to-all(f32[16,8,128]{2,1,0:T(8,128)S(1)} %get-tuple-element.26), channel_id=1, replica_groups={{11,12,13,14,15,0,1,2,3,4,5,6,7,8,9,10},{27,28,29,30,31,16,17,18,19,20,..., dimensions={0} | all-to-all | bytes 131072 | tf_op jit(solution)/shard_map/all_to_all | solution.py:288
  55.1 1.6 %norm.1 = (bf16[512,512]{1,0:T(8,128)(2,1)S(1)}, f32[512,128]{1,0:T(8,128)}) custom-call(f32[8,512]{1,0:T(8,128)S(1)} %get-tuple-element.32.aux_ref, bf16[512,512]{1,0:T(8,128)(2,1)S(1)} %copy-done.3, bf16[512,512]{1,0:T(8,128)(2,1)S(1)} %copy-done.2, f32[512,512]{1,0:T(8,128)S(1)} %get-tuple-element.25.att_ref, f32[16,8,128]{2,1,0:T(8,128)S(1)} %all_to_all.26.sums_ref), custom_call_target="tpu_custom_call" | custom-call | flops 134217728 | bytes 3145728 | tf_op jit(solution)/shard_map/norm/pallas_call | solution.py:273
  56.7 0.0 copy-start.4
  56.7 10.4 %all-to-all-start.3 = ((f32[32,16,128]{2,1,0:T(8,128)}), f32[32,16,128]{2,1,0:T(8,128)S(1)}, u32[]{:S(2)}, u32[]{:S(2)}) async-start(f32[32,16,128]{2,1,0:T(8,128)} %bitcast.3), calls=%async_computation.3 | async-start | bytes 524288 | tf_op jit(solution)/shard_map/all_to_all | solution.py:288
  67.1 4.4 %query.1 = (bf16[512,512]{1,0:T(8,128)(2,1)}, bf16[512,512]{1,0:T(8,128)(2,1)}) custom-call(f32[8,512]{1,0:T(8,128)S(1)} %get-tuple-element.32.aux_ref, bf16[512,512]{1,0:T(8,128)(2,1)} %k_ref.1, bf16[512,512]{1,0:T(8,128)(2,1)} %v_ref.1, bf16[512,512]{1,0:T(8,128)(2,1)S(1)} %get-tuple-element.27.d_ref, f32[512,128]{1,0:T(8,128)S(1)} %bitcast.6, ...), custom_call_target="tpu_custom_call" | custom-call | flops 536870912 | bytes 4194304 | tf_op jit(solution)/shard_map/query/pallas_call | solution.py:273
  71.6 0.0 copy-done.4
  71.6 2.3 %all-to-all-done.3.in_ref = f32[32,16,128]{2,1,0:T(8,128)S(1)} async-done(((f32[32,16,128]{2,1,0:T(8,128)}), f32[32,16,128]{2,1,0:T(8,128)S(1)}, u32[]{:S(2)}, u32[]{:S(2)}) %all-to-all-start.3) | async-done | bytes 262176 | tf_op jit(solution)/shard_map/all_to_all | solution.py:288
  73.8 0.8 scan.3
  74.6 9.4 %all-to-all-start.4 = ((f32[32,16,128]{2,1,0:T(8,128)}), f32[32,16,128]{2,1,0:T(8,128)S(1)}, u32[]{:S(2)}, u32[]{:S(2)}) async-start(f32[32,16,128]{2,1,0:T(8,128)} %scan.3), calls=%async_computation.4 | async-start | bytes 524288 | tf_op jit(solution)/shard_map/all_to_all | solution.py:288
  84.0 0.0 copy-start.5
  84.0 1.0 %copy-done.5 = bf16[512,512]{1,0:T(8,128)(2,1)S(1)} copy-done((bf16[512,512]{1,0:T(8,128)(2,1)S(1)}, bf16[512,512]{1,0:T(8,128)(2,1)}, u32[]{:S(2)}) %copy-start.5) | copy-done | bytes 524312
  85.0 0.0 copy-start
  85.0 0.0 copy-start.1
  85.1 5.6 %back.1 = (f32[512,512]{1,0:T(8,128)S(1)}, f32[512,512]{1,0:T(8,128)S(1)}) custom-call(f32[8,512]{1,0:T(8,128)S(1)} %get-tuple-element.32.aux_ref, bf16[512,512]{1,0:T(8,128)(2,1)} %q_hbm.3, bf16[512,512]{1,0:T(8,128)(2,1)} %k_ref.1, bf16[512,512]{1,0:T(8,128)(2,1)} %v_ref.1, bf16[512,512]{1,0:T(8,128)(2,1)S(1)} %copy-done.5), custom_call_target="tpu_custom_call" | custom-call | flops 1073741824 | bytes 4194304 | tf_op jit(solution)/shard_map/back/pallas_call | solution.py:273
  90.6 0.0 all-to-all-done.4
  90.6 0.0 copy-done
  90.7 0.0 copy-done.1
  90.7 1.6 %final.1 = (bf16[512,512]{1,0:T(8,128)(2,1)}, bf16[512,512]{1,0:T(8,128)(2,1)}) custom-call(f32[8,512]{1,0:T(8,128)S(1)} %get-tuple-element.32.aux_ref, bf16[512,512]{1,0:T(8,128)(2,1)S(1)} %copy-done, bf16[512,512]{1,0:T(8,128)(2,1)S(1)} %copy-done.1, f32[512,128]{1,0:T(8,128)S(1)} %bitcast.7, f32[512,512]{1,0:T(8,128)S(1)} %get-tuple-element.34.dk_ref, ...), custom_call_target="tpu_custom_call" | custom-call | flops 268435456 | bytes 5242880 | tf_op jit(solution)/shard_map/final/pallas_call | solution.py:273
Async XLA Ops:
  3.0 16.8 %all-to-all-start = ((f32[32,16,128]{2,1,0:T(8,128)}), f32[32,16,128]{2,1,0:T(8,128)S(1)}, u32[]{:S(2)}, u32[]{:S(2)}) async-start(f32[32,16,128]{2,1,0:T(8,128)} %bitcast.1), calls=%async_computation | async-start | bytes 524288 | tf_op jit(solution)/shard_map/all_to_all | solution.py:288
  15.4 0.7 copy-start.6
  19.8 13.5 %copy-start.2 = (bf16[512,512]{1,0:T(8,128)(2,1)S(1)}, bf16[512,512]{1,0:T(8,128)(2,1)}, u32[]{:S(2)}) copy-start(bf16[512,512]{1,0:T(8,128)(2,1)} %g_ref.3) | copy-start | bytes 1572868
  19.8 13.5 %copy-start.3 = (bf16[512,512]{1,0:T(8,128)(2,1)S(1)}, bf16[512,512]{1,0:T(8,128)(2,1)}, u32[]{:S(2)}) copy-start(bf16[512,512]{1,0:T(8,128)(2,1)} %q_hbm.3) | copy-start | bytes 1572868
  56.7 14.8 %copy-start.4 = (bf16[512,512]{1,0:T(8,128)(2,1)}, bf16[512,512]{1,0:T(8,128)(2,1)S(1)}, u32[]{:S(2)}) copy-start(bf16[512,512]{1,0:T(8,128)(2,1)S(1)} %get-tuple-element.27.d_ref) | copy-start | bytes 1572868
  56.7 17.1 %all-to-all-start.3 = ((f32[32,16,128]{2,1,0:T(8,128)}), f32[32,16,128]{2,1,0:T(8,128)S(1)}, u32[]{:S(2)}, u32[]{:S(2)}) async-start(f32[32,16,128]{2,1,0:T(8,128)} %bitcast.3), calls=%async_computation.3 | async-start | bytes 524288 | tf_op jit(solution)/shard_map/all_to_all | solution.py:288
  74.6 16.0 %all-to-all-start.4 = ((f32[32,16,128]{2,1,0:T(8,128)}), f32[32,16,128]{2,1,0:T(8,128)S(1)}, u32[]{:S(2)}, u32[]{:S(2)}) async-start(f32[32,16,128]{2,1,0:T(8,128)} %scan.3), calls=%async_computation.4 | async-start | bytes 524288 | tf_op jit(solution)/shard_map/all_to_all | solution.py:288
  84.0 1.0 %copy-start.5 = (bf16[512,512]{1,0:T(8,128)(2,1)S(1)}, bf16[512,512]{1,0:T(8,128)(2,1)}, u32[]{:S(2)}) copy-start(bf16[512,512]{1,0:T(8,128)(2,1)} %copy-done.4) | copy-start | bytes 1572868
  85.0 5.6 %copy-start = (bf16[512,512]{1,0:T(8,128)(2,1)S(1)}, bf16[512,512]{1,0:T(8,128)(2,1)}, u32[]{:S(2)}) copy-start(bf16[512,512]{1,0:T(8,128)(2,1)} %k_ref.1) | copy-start | bytes 1572868
  85.0 5.6 %copy-start.1 = (bf16[512,512]{1,0:T(8,128)(2,1)S(1)}, bf16[512,512]{1,0:T(8,128)(2,1)}, u32[]{:S(2)}) copy-start(bf16[512,512]{1,0:T(8,128)(2,1)} %v_ref.1) | copy-start | bytes 1572868

commit v6 on v5

--- a/solution.py
+++ b/solution.py
@@ -225,9 +225,11 @@
             ).astype(BF16)
 
 
-def back_kernel(aux_ref, q_hbm, k_hbm, v_hbm, d_ref, dk_ref, dv_ref, q_ref, k_ref, v_ref, sems):
+def back_kernel(
+    aux_ref, q_hbm, k_hbm, v_hbm, d_hbm, dk_ref, dv_ref, q_ref, k_ref, v_ref, d_ref, sems
+):
     count, width = q_ref.shape
-    wait(fetch(((q_hbm, q_ref), (k_hbm, k_ref), (v_hbm, v_ref)), sems))
+    wait(fetch(((q_hbm, q_ref), (k_hbm, k_ref), (v_hbm, v_ref), (d_hbm, d_ref)), sems))
     for h in range(width // DH):
         table = band(aux_ref[1:2, head(h)], count)
         for a in range(count // TILE):
@@ -352,10 +354,10 @@
     aux, normed, dq = lax.optimization_barrier((aux, normed, dq))
     suffix = scan(state, aux, heads, middle, True)
     dk, dv = call(
-        back_kernel, (shape(whole, F32), shape(whole, F32)), [VMEM] + [ANY] * 3 + [VMEM],
-        aux, far_q, far_k, far_v, grad,
+        back_kernel, (shape(whole, F32), shape(whole, F32)), [VMEM] + [ANY] * 4,
+        aux, far_q, far_k, far_v, pltpu.with_memory_space_constraint(grad, pltpu.HBM),
         name="back", flops=4 * pair, size=16 * unit,
-        scratch=[block, block, block, pltpu.SemaphoreType.DMA((3,))],
+        scratch=[block, block, block, block, pltpu.SemaphoreType.DMA((4,))],
     )
     dk, dv = call(
         final_kernel, (shape(whole, BF16), shape(whole, BF16)), [VMEM] * 6,

time: 92.8 us -> 92 us (level)
  local copies, waits for them, and re-layouts: 1.74 us -> 0.71 us
    unnamed x14 -> x12, local copies, waits for them, and re-layouts: 1.74 us -> 0.71 us
  transfers between devices with their start and end apart: 3 -> 3, of which waited for: 1 -> 2; matrix products, arithmetic and copies ran while one was open for 0% -> 0% of each run, Pallas kernels for 15% -> 15%
where the time goes in v6:
time: 92 us; the launch traced here: 91.5 us
  blocking collectives  34.6 us (38%)
  starting transfers between devices  32.2 us (35%)
  Pallas kernels  20.8 us (23%)
  waiting for transfers between devices  2.41 us (3%)
    all_to_all x2, blocking collectives, exchange(): lax.all_to_all(pieces, axis, 0, 0, tiled=True, axis_index_groups=[order])  34.6 us
    all_to_all x3, starting transfers between devices, exchange(): lax.all_to_all(pieces, axis, 0, 0, tiled=True, axis_index_groups=[order])  32.2 us
    pallas_call x9, Pallas kernels, call(): pl.pallas_call(kernel, out_shape=shapes, in_specs=specs, out_specs=out_sp...  20.8 us
    all_to_all x3, waiting for transfers between devices, exchange(): lax.all_to_all(pieces, axis, 0, 0, tiled=True, axis_index_groups=[order])  2.41 us
  transfers between devices with their start and end apart: 3, of which 2 were waited for; matrix products, arithmetic and copies ran while one was open for 0% of the time, Pallas kernels for 15%

profile of v6, /device:TPU:1, one launch (start us, length us, event | category | flops | bytes accessed | tf_op | source)
XLA Modules:
  0.0 91.5 jit_solution(11890497588300543396)
XLA Ops:
  0.6 2.3 %state.1 = (f32[512,128]{1,0:T(8,128)}, f32[8,512]{1,0:T(8,128)S(1)}) custom-call(f32[4]{0:T(128)} %rate_hbm.1, bf16[512,512]{1,0:T(8,128)(2,1)} %k_ref.1, bf16[512,512]{1,0:T(8,128)(2,1)} %v_ref.1), custom_call_target="tpu_custom_call" | custom-call | flops 134217728 | bytes 1048576 | tf_op jit(solution)/shard_map/state/pallas_call | solution.py:275
  3.0 12.5 %all-to-all-start = ((f32[32,16,128]{2,1,0:T(8,128)}), f32[32,16,128]{2,1,0:T(8,128)S(1)}, u32[]{:S(2)}, u32[]{:S(2)}) async-start(f32[32,16,128]{2,1,0:T(8,128)} %bitcast.1), calls=%async_computation | async-start | bytes 524288 | tf_op jit(solution)/shard_map/all_to_all | solution.py:290
  15.4 0.0 copy-start.5
  15.4 0.7 copy-done.5
  16.1 3.7 %inner.1 = (f32[512,512]{1,0:T(8,128)S(1)}, f32[8,512]{1,0:T(8,128)S(1)}) custom-call(f32[8,512]{1,0:T(8,128)S(1)} %get-tuple-element.21.rows_ref, f32[1,512]{1,0:T(1,128)S(1)} %bitcast.8, bf16[512,512]{1,0:T(8,128)(2,1)} %q_hbm.3, bf16[512,512]{1,0:T(8,128)(2,1)} %k_ref.1, bf16[512,512]{1,0:T(8,128)(2,1)} %v_ref.1), custom_call_target="tpu_custom_call" | custom-call | flops 536870912 | bytes 2621440 | tf_op jit(solution)/shard_map/inner/pallas_call | solution.py:275
  19.8 0.0 all-to-all-done.in_ref
  19.8 0.0 copy-start.2
  19.8 0.0 copy-start.3
  19.8 0.1 scan.2
  19.9 13.4 %all_to_all.25 = f32[32,16,128]{2,1,0:T(8,128)S(1)} all-to-all(f32[32,16,128]{2,1,0:T(8,128)S(1)} %scan.2), channel_id=1, replica_groups={{288,304,320,336,352,368,384,400,416,432,448,464,480,496,0,16,32,48,64,..., dimensions={0} | all-to-all | bytes 524288 | tf_op jit(solution)/shard_map/all_to_all | solution.py:290
  33.3 0.0 copy-done.2
  33.3 0.0 copy-done.3
  33.3 0.6 attend.1
  33.9 21.2 %all_to_all.26.sums_ref = f32[16,8,128]{2,1,0:T(8,128)S(1)} all-to-all(f32[16,8,128]{2,1,0:T(8,128)S(1)} %get-tuple-element.26), channel_id=1, replica_groups={{11,12,13,14,15,0,1,2,3,4,5,6,7,8,9,10},{27,28,29,30,31,16,17,18,19,20,..., dimensions={0} | all-to-all | bytes 131072 | tf_op jit(solution)/shard_map/all_to_all | solution.py:290
  55.1 1.6 %norm.1 = (bf16[512,512]{1,0:T(8,128)(2,1)S(1)}, f32[512,128]{1,0:T(8,128)}) custom-call(f32[8,512]{1,0:T(8,128)S(1)} %get-tuple-element.32.aux_ref, bf16[512,512]{1,0:T(8,128)(2,1)S(1)} %copy-done.3, bf16[512,512]{1,0:T(8,128)(2,1)S(1)} %copy-done.2, f32[512,512]{1,0:T(8,128)S(1)} %get-tuple-element.25.att_ref, f32[16,8,128]{2,1,0:T(8,128)S(1)} %all_to_all.26.sums_ref), custom_call_target="tpu_custom_call" | custom-call | flops 134217728 | bytes 3145728 | tf_op jit(solution)/shard_map/norm/pallas_call | solution.py:275
  56.7 0.0 copy-start.4
  56.7 10.4 %all-to-all-start.3 = ((f32[32,16,128]{2,1,0:T(8,128)}), f32[32,16,128]{2,1,0:T(8,128)S(1)}, u32[]{:S(2)}, u32[]{:S(2)}) async-start(f32[32,16,128]{2,1,0:T(8,128)} %bitcast.3), calls=%async_computation.3 | async-start | bytes 524288 | tf_op jit(solution)/shard_map/all_to_all | solution.py:290
  67.1 4.4 %query.1 = (bf16[512,512]{1,0:T(8,128)(2,1)}, bf16[512,512]{1,0:T(8,128)(2,1)}) custom-call(f32[8,512]{1,0:T(8,128)S(1)} %get-tuple-element.32.aux_ref, bf16[512,512]{1,0:T(8,128)(2,1)} %k_ref.1, bf16[512,512]{1,0:T(8,128)(2,1)} %v_ref.1, bf16[512,512]{1,0:T(8,128)(2,1)S(1)} %get-tuple-element.27.d_ref.d_hbm, f32[512,128]{1,0:T(8,128)S(1)} %bitcast.6, ...), custom_call_target="tpu_custom_call" | custom-call | flops 536870912 | bytes 4194304 | tf_op jit(solution)/shard_map/query/pallas_call | solution.py:275
  71.6 0.0 copy-done.4
  71.6 2.3 %all-to-all-done.3.in_ref = f32[32,16,128]{2,1,0:T(8,128)S(1)} async-done(((f32[32,16,128]{2,1,0:T(8,128)}), f32[32,16,128]{2,1,0:T(8,128)S(1)}, u32[]{:S(2)}, u32[]{:S(2)}) %all-to-all-start.3) | async-done | bytes 262176 | tf_op jit(solution)/shard_map/all_to_all | solution.py:290
  73.8 0.8 scan.3
  74.6 9.4 %all-to-all-start.4 = ((f32[32,16,128]{2,1,0:T(8,128)}), f32[32,16,128]{2,1,0:T(8,128)S(1)}, u32[]{:S(2)}, u32[]{:S(2)}) async-start(f32[32,16,128]{2,1,0:T(8,128)} %scan.3), calls=%async_computation.4 | async-start | bytes 524288 | tf_op jit(solution)/shard_map/all_to_all | solution.py:290
  84.0 0.0 copy-start
  84.0 0.0 copy-start.1
  84.0 5.7 %back.1 = (f32[512,512]{1,0:T(8,128)S(1)}, f32[512,512]{1,0:T(8,128)S(1)}) custom-call(f32[8,512]{1,0:T(8,128)S(1)} %get-tuple-element.32.aux_ref, bf16[512,512]{1,0:T(8,128)(2,1)} %q_hbm.3, bf16[512,512]{1,0:T(8,128)(2,1)} %k_ref.1, bf16[512,512]{1,0:T(8,128)(2,1)} %v_ref.1, bf16[512,512]{1,0:T(8,128)(2,1)} %copy-done.4), custom_call_target="tpu_custom_call" | custom-call | flops 1073741824 | bytes 4194304 | tf_op jit(solution)/shard_map/back/pallas_call | solution.py:275
  89.8 0.1 all-to-all-done.4
  89.9 0.0 copy-done
  89.9 0.0 copy-done.1
  89.9 1.6 %final.1 = (bf16[512,512]{1,0:T(8,128)(2,1)}, bf16[512,512]{1,0:T(8,128)(2,1)}) custom-call(f32[8,512]{1,0:T(8,128)S(1)} %get-tuple-element.32.aux_ref, bf16[512,512]{1,0:T(8,128)(2,1)S(1)} %copy-done, bf16[512,512]{1,0:T(8,128)(2,1)S(1)} %copy-done.1, f32[512,128]{1,0:T(8,128)S(1)} %bitcast.7, f32[512,512]{1,0:T(8,128)S(1)} %get-tuple-element.34.dk_ref, ...), custom_call_target="tpu_custom_call" | custom-call | flops 268435456 | bytes 5242880 | tf_op jit(solution)/shard_map/final/pallas_call | solution.py:275
Async XLA Ops:
  3.0 16.8 %all-to-all-start = ((f32[32,16,128]{2,1,0:T(8,128)}), f32[32,16,128]{2,1,0:T(8,128)S(1)}, u32[]{:S(2)}, u32[]{:S(2)}) async-start(f32[32,16,128]{2,1,0:T(8,128)} %bitcast.1), calls=%async_computation | async-start | bytes 524288 | tf_op jit(solution)/shard_map/all_to_all | solution.py:290
  15.4 0.7 copy-start.5
  19.8 13.5 %copy-start.2 = (bf16[512,512]{1,0:T(8,128)(2,1)S(1)}, bf16[512,512]{1,0:T(8,128)(2,1)}, u32[]{:S(2)}) copy-start(bf16[512,512]{1,0:T(8,128)(2,1)} %g_ref.3) | copy-start | bytes 1572868
  19.8 13.5 %copy-start.3 = (bf16[512,512]{1,0:T(8,128)(2,1)S(1)}, bf16[512,512]{1,0:T(8,128)(2,1)}, u32[]{:S(2)}) copy-start(bf16[512,512]{1,0:T(8,128)(2,1)} %q_hbm.3) | copy-start | bytes 1572868
  56.7 14.8 %copy-start.4 = (bf16[512,512]{1,0:T(8,128)(2,1)}, bf16[512,512]{1,0:T(8,128)(2,1)S(1)}, u32[]{:S(2)}) copy-start(bf16[512,512]{1,0:T(8,128)(2,1)S(1)} %get-tuple-element.27.d_ref.d_hbm) | copy-start | bytes 1572868
  56.7 17.1 %all-to-all-start.3 = ((f32[32,16,128]{2,1,0:T(8,128)}), f32[32,16,128]{2,1,0:T(8,128)S(1)}, u32[]{:S(2)}, u32[]{:S(2)}) async-start(f32[32,16,128]{2,1,0:T(8,128)} %bitcast.3), calls=%async_computation.3 | async-start | bytes 524288 | tf_op jit(solution)/shard_map/all_to_all | solution.py:290
  74.6 15.3 %all-to-all-start.4 = ((f32[32,16,128]{2,1,0:T(8,128)}), f32[32,16,128]{2,1,0:T(8,128)S(1)}, u32[]{:S(2)}, u32[]{:S(2)}) async-start(f32[32,16,128]{2,1,0:T(8,128)} %scan.3), calls=%async_computation.4 | async-start | bytes 524288 | tf_op jit(solution)/shard_map/all_to_all | solution.py:290
  84.0 5.9 %copy-start = (bf16[512,512]{1,0:T(8,128)(2,1)S(1)}, bf16[512,512]{1,0:T(8,128)(2,1)}, u32[]{:S(2)}) copy-start(bf16[512,512]{1,0:T(8,128)(2,1)} %k_ref.1) | copy-start | bytes 1572868
  84.0 5.9 %copy-start.1 = (bf16[512,512]{1,0:T(8,128)(2,1)S(1)}, bf16[512,512]{1,0:T(8,128)(2,1)}, u32[]{:S(2)}) copy-start(bf16[512,512]{1,0:T(8,128)(2,1)} %v_ref.1) | copy-start | bytes 1572868

commit v7 on v6

--- a/solution.py
+++ b/solution.py
@@ -200,11 +200,11 @@
 
 
 def query_kernel(
-    total, aux_ref, k_hbm, v_hbm, d_ref, prefix_ref, att_ref, sums_ref,
-    normed_ref, dq_ref, k_ref, v_ref, sems,
+    total, aux_ref, q_hbm, k_hbm, v_hbm, d_ref, prefix_ref, att_ref, sums_ref,
+    normed_ref, dq_ref, dk_ref, dv_ref, q_ref, k_ref, v_ref, sems,
 ):
     count, width = k_ref.shape
-    copies = fetch(((k_hbm, k_ref), (v_hbm, v_ref)), sems)
+    copies = fetch(((q_hbm, q_ref), (k_hbm, k_ref), (v_hbm, v_ref)), sems)
     rinv, _, tiles = norm_scales(total, sums_ref)
     rinv = to_columns(rinv, 0, tiles)
     for h in range(width // DH):
@@ -223,6 +223,26 @@
             dq_ref[here, head(h)] = (
                 dot(grads, k_ref[:seen, head(h)], NN) + past[here, :]
             ).astype(BF16)
+        if h == 0:
+            pair_grads(table, q_ref, k_ref, v_ref, d_ref, head(0), dk_ref, dv_ref, head(0))
+
+
+def pair_grads(table, q_ref, k_ref, v_ref, d_ref, at, dk_ref, dv_ref, to):
+    count = q_ref.shape[0]
+    for a in range(count // TILE):
+        here = slice(a * TILE, (a + 1) * TILE)
+        seen = (a + 1) * TILE
+        part = table[:, count - seen :]
+        q, d = q_ref[here, at], d_ref[here, at]
+        weights = (dot(q, k_ref[:seen, at], NT) * part).astype(BF16)
+        grads = (dot(d, v_ref[:seen, at], NT) * part).astype(BF16)
+        dk, dv = dot(grads, q, TN), dot(weights, d, TN)
+        if a:
+            before = slice(0, a * TILE)
+            dk_ref[before, to] += dk[before, :]
+            dv_ref[before, to] += dv[before, :]
+        dk_ref[here, to] = dk[here, :]
+        dv_ref[here, to] = dv[here, :]
 
 
 def back_kernel(
@@ -230,26 +250,13 @@
 ):
     count, width = q_ref.shape
     wait(fetch(((q_hbm, q_ref), (k_hbm, k_ref), (v_hbm, v_ref), (d_hbm, d_ref)), sems))
-    for h in range(width // DH):
+    for h in range(1, width // DH):
         table = band(aux_ref[1:2, head(h)], count)
-        for a in range(count // TILE):
-            here = slice(a * TILE, (a + 1) * TILE)
-            seen = (a + 1) * TILE
-            part = table[:, count - seen :]
-            q, d = q_ref[here, head(h)], d_ref[here, head(h)]
-            weights = (dot(q, k_ref[:seen, head(h)], NT) * part).astype(BF16)
-            grads = (dot(d, v_ref[:seen, head(h)], NT) * part).astype(BF16)
-            dk, dv = dot(grads, q, TN), dot(weights, d, TN)
-            if a:
-                before = slice(0, a * TILE)
-                dk_ref[before, head(h)] += dk[before, :]
-                dv_ref[before, head(h)] += dv[before, :]
-            dk_ref[here, head(h)] = dk[here, :]
-            dv_ref[here, head(h)] = dv[here, :]
+        pair_grads(table, q_ref, k_ref, v_ref, d_ref, head(h), dk_ref, dv_ref, head(h - 1))
 
 
 def final_kernel(
-    aux_ref, k_ref, v_ref, suffix_ref, dk_ref, dv_ref, kout_hbm, vout_hbm, kout_ref, vout_ref, sems
+    aux_ref, k_ref, v_ref, suffix_ref, dk0_ref, dv0_ref, dk_ref, dv_ref, kout_hbm, vout_hbm, kout_ref, vout_ref, sems
 ):
     count, width = k_ref.shape
     copies = []
@@ -257,10 +264,10 @@
         tail = falling(aux_ref[1:2, head(h)], count, 1.0)
         suffix = suffix_ref[head(h), :]
         kout_ref[:, head(h)] = (
-            dk_ref[:, head(h)] + dot_wide(v_ref[:, head(h)], suffix.T) * tail
+            (dk_ref[:, head(h - 1)] if h else dk0_ref[...]) + dot_wide(v_ref[:, head(h)], suffix.T) * tail
         ).astype(BF16)
         vout_ref[:, head(h)] = (
-            dv_ref[:, head(h)] + dot_wide(k_ref[:, head(h)], suffix) * tail
+            (dv_ref[:, head(h - 1)] if h else dv0_ref[...]) + dot_wide(k_ref[:, head(h)], suffix) * tail
         ).astype(BF16)
         for index, (held, out) in enumerate(((kout_ref, kout_hbm), (vout_ref, vout_hbm))):
             copy = pltpu.make_async_copy(
@@ -344,24 +351,25 @@
         aux, queries, out_grad, attended, sums,
         name="norm", flops=wide, size=12 * unit,
     )
-    normed, dq = call(
+    one, rest = shape((count, DH), F32), shape((count, width - DH), F32)
+    normed, dq, dk0, dv0 = call(
         functools.partial(query_kernel, total),
-        (shape(whole, BF16), shape(whole, BF16)), [VMEM] + [ANY] * 2 + [VMEM] * 4,
-        aux, far_k, far_v, grad, prefix, attended, sums,
+        (shape(whole, BF16), shape(whole, BF16), one, one), [VMEM] + [ANY] * 3 + [VMEM] * 4,
+        aux, far_q, far_k, far_v, grad, prefix, attended, sums,
         name="query", flops=2 * pair, size=16 * unit,
-        scratch=[block, block, pltpu.SemaphoreType.DMA((2,))],
+        scratch=[block, block, block, pltpu.SemaphoreType.DMA((3,))],
     )
     aux, normed, dq = lax.optimization_barrier((aux, normed, dq))
     suffix = scan(state, aux, heads, middle, True)
     dk, dv = call(
-        back_kernel, (shape(whole, F32), shape(whole, F32)), [VMEM] + [ANY] * 4,
+        back_kernel, (rest, rest), [VMEM] + [ANY] * 4,
         aux, far_q, far_k, far_v, pltpu.with_memory_space_constraint(grad, pltpu.HBM),
         name="back", flops=4 * pair, size=16 * unit,
         scratch=[block, block, block, block, pltpu.SemaphoreType.DMA((4,))],
     )
     dk, dv = call(
-        final_kernel, (shape(whole, BF16), shape(whole, BF16)), [VMEM] * 6,
-        aux, keys, values, suffix, dk, dv,
+        final_kernel, (shape(whole, BF16), shape(whole, BF16)), [VMEM] * 8,
+        aux, keys, values, suffix, dk0, dv0, dk, dv,
         name="final", flops=2 * wide, size=20 * unit, out_specs=(ANY, ANY),
         scratch=[block, block, pltpu.SemaphoreType.DMA((2 * heads,))],
     )

time: 92 us -> 92 us (level)
  no operation moved by 1% of the time
where the time goes in v7:
time: 92 us; the launch traced here: 91.5 us
  blocking collectives  34.6 us (38%)
  starting transfers between devices  32.2 us (35%)
  Pallas kernels  21.1 us (23%)
  waiting for transfers between devices  2.07 us (2%)
    all_to_all x2, blocking collectives, exchange(): lax.all_to_all(pieces, axis, 0, 0, tiled=True, axis_index_groups=[order])  34.6 us
    all_to_all x3, starting transfers between devices, exchange(): lax.all_to_all(pieces, axis, 0, 0, tiled=True, axis_index_groups=[order])  32.2 us
    pallas_call x9, Pallas kernels, call(): pl.pallas_call(kernel, out_shape=shapes, in_specs=specs, out_specs=out_sp...  21.1 us
    all_to_all x3, waiting for transfers between devices, exchange(): lax.all_to_all(pieces, axis, 0, 0, tiled=True, axis_index_groups=[order])  2.07 us
  transfers between devices with their start and end apart: 3, of which 2 were waited for; matrix products, arithmetic and copies ran while one was open for 0% of the time, Pallas kernels for 15%

profile of v7, /device:TPU:1, one launch (start us, length us, event | category | flops | bytes accessed | tf_op | source)
XLA Modules:
  0.0 91.5 jit_solution(17714300469684994506)
XLA Ops:
  0.6 2.3 %state.1 = (f32[512,128]{1,0:T(8,128)}, f32[8,512]{1,0:T(8,128)S(1)}) custom-call(f32[4]{0:T(128)} %rate_hbm.1, bf16[512,512]{1,0:T(8,128)(2,1)} %k_ref.1, bf16[512,512]{1,0:T(8,128)(2,1)} %v_ref.1), custom_call_target="tpu_custom_call" | custom-call | flops 134217728 | bytes 1048576 | tf_op jit(solution)/shard_map/state/pallas_call | solution.py:282
  3.0 12.5 %all-to-all-start = ((f32[32,16,128]{2,1,0:T(8,128)}), f32[32,16,128]{2,1,0:T(8,128)S(1)}, u32[]{:S(2)}, u32[]{:S(2)}) async-start(f32[32,16,128]{2,1,0:T(8,128)} %bitcast.1), calls=%async_computation | async-start | bytes 524288 | tf_op jit(solution)/shard_map/all_to_all | solution.py:297
  15.4 0.0 copy-start.9
  15.4 0.7 copy-done.9
  16.1 3.7 %inner.1 = (f32[512,512]{1,0:T(8,128)S(1)}, f32[8,512]{1,0:T(8,128)S(1)}) custom-call(f32[8,512]{1,0:T(8,128)S(1)} %get-tuple-element.23.rows_ref, f32[1,512]{1,0:T(1,128)S(1)} %bitcast.8, bf16[512,512]{1,0:T(8,128)(2,1)} %q_hbm.5, bf16[512,512]{1,0:T(8,128)(2,1)} %k_ref.1, bf16[512,512]{1,0:T(8,128)(2,1)} %v_ref.1), custom_call_target="tpu_custom_call" | custom-call | flops 536870912 | bytes 2621440 | tf_op jit(solution)/shard_map/inner/pallas_call | solution.py:282
  19.8 0.0 all-to-all-done.in_ref
  19.8 0.0 copy-start
  19.8 0.0 copy-start.3
  19.8 0.1 scan.2
  19.9 13.4 %all_to_all.25 = f32[32,16,128]{2,1,0:T(8,128)S(1)} all-to-all(f32[32,16,128]{2,1,0:T(8,128)S(1)} %scan.2), channel_id=1, replica_groups={{288,304,320,336,352,368,384,400,416,432,448,464,480,496,0,16,32,48,64,..., dimensions={0} | all-to-all | bytes 524288 | tf_op jit(solution)/shard_map/all_to_all | solution.py:297
  33.3 0.0 copy-done
  33.3 0.0 copy-done.3
  33.3 0.6 attend.1
  33.9 21.2 %all_to_all.26.sums_ref = f32[16,8,128]{2,1,0:T(8,128)S(1)} all-to-all(f32[16,8,128]{2,1,0:T(8,128)S(1)} %get-tuple-element.28), channel_id=1, replica_groups={{11,12,13,14,15,0,1,2,3,4,5,6,7,8,9,10},{27,28,29,30,31,16,17,18,19,20,..., dimensions={0} | all-to-all | bytes 131072 | tf_op jit(solution)/shard_map/all_to_all | solution.py:297
  55.1 1.6 %norm.1 = (bf16[512,512]{1,0:T(8,128)(2,1)S(1)}, f32[512,128]{1,0:T(8,128)}) custom-call(f32[8,512]{1,0:T(8,128)S(1)} %get-tuple-element.34.aux_ref, bf16[512,512]{1,0:T(8,128)(2,1)S(1)} %copy-done, bf16[512,512]{1,0:T(8,128)(2,1)S(1)} %copy-done.3, f32[512,512]{1,0:T(8,128)S(1)} %get-tuple-element.27.att_ref, f32[16,8,128]{2,1,0:T(8,128)S(1)} %all_to_all.26.sums_ref), custom_call_target="tpu_custom_call" | custom-call | flops 134217728 | bytes 3145728 | tf_op jit(solution)/shard_map/norm/pallas_call | solution.py:282
  56.7 0.0 copy-start.4
  56.7 10.4 %all-to-all-start.3 = ((f32[32,16,128]{2,1,0:T(8,128)}), f32[32,16,128]{2,1,0:T(8,128)S(1)}, u32[]{:S(2)}, u32[]{:S(2)}) async-start(f32[32,16,128]{2,1,0:T(8,128)} %bitcast.3), calls=%async_computation.3 | async-start | bytes 524288 | tf_op jit(solution)/shard_map/all_to_all | solution.py:297
  67.1 5.7 %query.1 = (bf16[512,512]{1,0:T(8,128)(2,1)}, bf16[512,512]{1,0:T(8,128)(2,1)}, f32[512,128]{1,0:T(8,128)S(1)}, f32[512,128]{1,0:T(8,128)S(1)}) custom-call(f32[8,512]{1,0:T(8,128)S(1)} %get-tuple-element.34.aux_ref, bf16[512,512]{1,0:T(8,128)(2,1)} %q_hbm.5, bf16[512,512]{1,0:T(8,128)(2,1)} %k_ref.1, bf16[512,512]{1,0:T(8,128)(2,1)} %v_ref.1, ...), custom_call_target="tpu_custom_call" | custom-call | flops 536870912 | bytes 4194304 | tf_op jit(solution)/shard_map/query/pallas_call | solution.py:282
  72.8 0.0 copy-done.4
  72.8 0.0 copy-start.5
  72.8 0.0 copy-start.7
  72.8 1.0 %all-to-all-done.3.in_ref = f32[32,16,128]{2,1,0:T(8,128)S(1)} async-done(((f32[32,16,128]{2,1,0:T(8,128)}), f32[32,16,128]{2,1,0:T(8,128)S(1)}, u32[]{:S(2)}, u32[]{:S(2)}) %all-to-all-start.3) | async-done | bytes 262176 | tf_op jit(solution)/shard_map/all_to_all | solution.py:297
  73.8 0.8 scan.3
  74.6 0.0 copy-done.5
  74.6 0.0 copy-done.7
  74.6 9.4 %all-to-all-start.4 = ((f32[32,16,128]{2,1,0:T(8,128)}), f32[32,16,128]{2,1,0:T(8,128)S(1)}, u32[]{:S(2)}, u32[]{:S(2)}) async-start(f32[32,16,128]{2,1,0:T(8,128)} %scan.3), calls=%async_computation.4 | async-start | bytes 524288 | tf_op jit(solution)/shard_map/all_to_all | solution.py:297
  84.0 0.0 copy-start.1
  84.0 0.0 copy-start.2
  84.0 0.0 copy-start.6
  84.0 0.0 copy-start.8
  84.0 4.8 %back.1 = (f32[512,384]{1,0:T(8,128)S(1)}, f32[512,384]{1,0:T(8,128)S(1)}) custom-call(f32[8,512]{1,0:T(8,128)S(1)} %get-tuple-element.34.aux_ref, bf16[512,512]{1,0:T(8,128)(2,1)} %q_hbm.5, bf16[512,512]{1,0:T(8,128)(2,1)} %k_ref.1, bf16[512,512]{1,0:T(8,128)(2,1)} %v_ref.1, bf16[512,512]{1,0:T(8,128)(2,1)} %copy-done.4), custom_call_target="tpu_custom_call" | custom-call | flops 1073741824 | bytes 4194304 | tf_op jit(solution)/shard_map/back/pallas_call | solution.py:282
  88.8 1.1 %all-to-all-done.4 = f32[32,16,128]{2,1,0:T(8,128)S(1)} async-done(((f32[32,16,128]{2,1,0:T(8,128)}), f32[32,16,128]{2,1,0:T(8,128)S(1)}, u32[]{:S(2)}, u32[]{:S(2)}) %all-to-all-start.4) | async-done | bytes 262176 | tf_op jit(solution)/shard_map/all_to_all | solution.py:297
  89.9 0.0 copy-done.1
  89.9 0.0 copy-done.2
  89.9 0.0 copy-done.6
  89.9 0.0 copy-done.8
  89.9 1.6 %final.1 = (bf16[512,512]{1,0:T(8,128)(2,1)}, bf16[512,512]{1,0:T(8,128)(2,1)}) custom-call(f32[8,512]{1,0:T(8,128)S(1)} %get-tuple-element.34.aux_ref, bf16[512,512]{1,0:T(8,128)(2,1)S(1)} %copy-done.1, bf16[512,512]{1,0:T(8,128)(2,1)S(1)} %copy-done.2, f32[512,128]{1,0:T(8,128)S(1)} %bitcast.7, f32[512,128]{1,0:T(8,128)S(1)} %copy-done.6, ...), custom_call_target="tpu_custom_call" | custom-call | flops 268435456 | bytes 5242880 | tf_op jit(solution)/shard_map/final/pallas_call | solution.py:282
Async XLA Ops:
  3.0 16.8 %all-to-all-start = ((f32[32,16,128]{2,1,0:T(8,128)}), f32[32,16,128]{2,1,0:T(8,128)S(1)}, u32[]{:S(2)}, u32[]{:S(2)}) async-start(f32[32,16,128]{2,1,0:T(8,128)} %bitcast.1), calls=%async_computation | async-start | bytes 524288 | tf_op jit(solution)/shard_map/all_to_all | solution.py:297
  15.4 0.7 copy-start.9
  19.8 13.5 %copy-start = (bf16[512,512]{1,0:T(8,128)(2,1)S(1)}, bf16[512,512]{1,0:T(8,128)(2,1)}, u32[]{:S(2)}) copy-start(bf16[512,512]{1,0:T(8,128)(2,1)} %q_hbm.5) | copy-start | bytes 1572868
  19.8 13.5 %copy-start.3 = (bf16[512,512]{1,0:T(8,128)(2,1)S(1)}, bf16[512,512]{1,0:T(8,128)(2,1)}, u32[]{:S(2)}) copy-start(bf16[512,512]{1,0:T(8,128)(2,1)} %g_ref.3) | copy-start | bytes 1572868
  56.7 16.1 %copy-start.4 = (bf16[512,512]{1,0:T(8,128)(2,1)}, bf16[512,512]{1,0:T(8,128)(2,1)S(1)}, u32[]{:S(2)}) copy-start(bf16[512,512]{1,0:T(8,128)(2,1)S(1)} %get-tuple-element.29.d_ref.d_hbm) | copy-start | bytes 1572868
  56.7 17.1 %all-to-all-start.3 = ((f32[32,16,128]{2,1,0:T(8,128)}), f32[32,16,128]{2,1,0:T(8,128)S(1)}, u32[]{:S(2)}, u32[]{:S(2)}) async-start(f32[32,16,128]{2,1,0:T(8,128)} %bitcast.3), calls=%async_computation.3 | async-start | bytes 524288 | tf_op jit(solution)/shard_map/all_to_all | solution.py:297
  72.8 1.8 %copy-start.5 = (f32[512,128]{1,0:T(8,128)}, f32[512,128]{1,0:T(8,128)S(1)}, u32[]{:S(2)}) copy-start(f32[512,128]{1,0:T(8,128)S(1)} %get-tuple-element.36.dk0_ref) | copy-start | bytes 786436
  72.8 1.8 %copy-start.7 = (f32[512,128]{1,0:T(8,128)}, f32[512,128]{1,0:T(8,128)S(1)}, u32[]{:S(2)}) copy-start(f32[512,128]{1,0:T(8,128)S(1)} %get-tuple-element.37.dv0_ref) | copy-start | bytes 786436
  74.6 15.3 %all-to-all-start.4 = ((f32[32,16,128]{2,1,0:T(8,128)}), f32[32,16,128]{2,1,0:T(8,128)S(1)}, u32[]{:S(2)}, u32[]{:S(2)}) async-start(f32[32,16,128]{2,1,0:T(8,128)} %scan.3), calls=%async_computation.4 | async-start | bytes 524288 | tf_op jit(solution)/shard_map/all_to_all | solution.py:297
  84.0 5.9 %copy-start.1 = (bf16[512,512]{1,0:T(8,128)(2,1)S(1)}, bf16[512,512]{1,0:T(8,128)(2,1)}, u32[]{:S(2)}) copy-start(bf16[512,512]{1,0:T(8,128)(2,1)} %k_ref.1) | copy-start | bytes 1572868
  84.0 5.9 %copy-start.2 = (bf16[512,512]{1,0:T(8,128)(2,1)S(1)}, bf16[512,512]{1,0:T(8,128)(2,1)}, u32[]{:S(2)}) copy-start(bf16[512,512]{1,0:T(8,128)(2,1)} %v_ref.1) | copy-start | bytes 1572868
  84.0 5.9 %copy-start.6 = (f32[512,128]{1,0:T(8,128)S(1)}, f32[512,128]{1,0:T(8,128)}, u32[]{:S(2)}) copy-start(f32[512,128]{1,0:T(8,128)} %copy-done.5) | copy-start | bytes 786436
  84.0 5.9 %copy-start.8 = (f32[512,128]{1,0:T(8,128)S(1)}, f32[512,128]{1,0:T(8,128)}, u32[]{:S(2)}) copy-start(f32[512,128]{1,0:T(8,128)} %copy-done.7) | copy-start | bytes 786436
